TPU v7x, 32 devices: a whole 2x2x4 slice. The times are simulated.
32 devices in a mesh: frames: 4 (over y, x), rows: 8 (over z, core).
Axes of the slice: x: 2, y: 2, z: 4, core: 2. Of those that a mesh axis runs over, the one named last changes fastest.
Arguments:
- kspace: float32 [2, 16, 128, 2, 128], P(None, 'frames', 'rows'), may hold values from -6 to 6
- line_mask: int32 [2, 16, 128], P(None, 'frames', 'rows'), may hold values from 0 to 1
- valid_flags: int32 [2, 16], P(None, 'frames'), may hold values from 0 to 1
- target: float32 [2, 16, 128, 2, 128], P(None, 'frames', 'rows')
- conv_in: float32 [1, 216, 64], P(None, None, 'rows'), may hold values from -0.4375 to 0.4375
- conv_mid: float32 [1, 1, 1728, 64], P(None, None, None, 'rows')
- conv_out: float32 [1, 2, 1728], P(None, None, 'rows')
- conv_bias: float32 [1, 2, 64], P(None, None, 'rows'), may hold values from -1 to 1
- first_in: float32 [1, 216, 64], P(None, None, 'rows'), may hold values from -9.1552734e-05 to 9.1552734e-05
- first_mid: float32 [1, 1, 1728, 64], P(None, None, None, 'rows'), may hold values from -9.1552734e-05 to 9.1552734e-05
- first_out: float32 [1, 2, 1728], P(None, None, 'rows'), may hold values from -9.1552734e-05 to 9.1552734e-05
- first_bias: float32 [1, 2, 64], P(None, None, 'rows'), may hold values from -0.00036621094 to 0.00036621094
- second_in: float32 [1, 216, 64], P(None, None, 'rows'), may hold values from 1.25e-12 to 5e-12
- second_mid: float32 [1, 1, 1728, 64], P(None, None, None, 'rows'), may hold values from 1.953125e-11 to 7.8125e-11
- second_out: float32 [1, 2, 1728], P(None, None, 'rows'), may hold values from 1.953125e-11 to 7.8125e-11
- second_bias: float32 [1, 2, 64], P(None, None, 'rows'), may hold values from 3.125e-10 to 1.25e-09
Outputs:
- loss_sum: float32 [], replicated
- valid_count: float32 [], replicated
- grad_norm: float32 [], replicated
- moment_in: float32 [1, 216, 64], P(None, None, 'rows')
- moment_mid: float32 [1, 1, 1728, 64], P(None, None, None, 'rows')
- moment_out: float32 [1, 2, 1728], P(None, None, 'rows')
- moment_bias: float32 [1, 2, 64], P(None, None, 'rows')
- square_in: float32 [1, 216, 64], P(None, None, 'rows')
- square_mid: float32 [1, 1, 1728, 64], P(None, None, None, 'rows')
- square_out: float32 [1, 2, 1728], P(None, None, 'rows')
- square_bias: float32 [1, 2, 64], P(None, None, 'rows')
- master_in: float32 [1, 216, 64], P(None, None, 'rows')
- master_mid: float32 [1, 1, 1728, 64], P(None, None, None, 'rows')
- master_out: float32 [1, 2, 1728], P(None, None, 'rows')
- master_bias: float32 [1, 2, 64], P(None, None, 'rows')
- copy_in: bfloat16 [1, 216, 64], P(None, None, 'rows')
- copy_mid: bfloat16 [1, 1, 1728, 64], P(None, None, None, 'rows')
- copy_out: bfloat16 [1, 2, 1728], P(None, None, 'rows')
- copy_bias: bfloat16 [1, 2, 64], P(None, None, 'rows')
All inputs are finite; a program needn't handle non-finite values.
Results may differ from a plain program's by a relative error of at most 0.0085.
Values may be sent and summed in bfloat16 or wider, within the bound.
No kernel may reach another device: no remote copies, remote signals or barrier semaphores. Data moves between devices by JAX's collectives and lax.ppermute only.
A program may use at most 128 MiB of HBM per device.

v0:
```python
import jax
import jax.numpy as jnp
import ml_dtypes
import numpy as np
from jax import lax
from jax.experimental import pallas as pl
from jax.experimental.pallas import tpu as pltpu
from jax.sharding import Mesh
from jax.sharding import PartitionSpec as P

NX = 128
CAS = 1
MIDS = 1
STEP = 10


CLIP = 0.05
RATE = 0.03
BETA_ONE = 0.9
BETA_TWO = 0.999
EPSILON = 1e-08
DECAY = 0.01
HIGHEST = lax.Precision.HIGHEST


def with_halo(shard, sides, width):
    for axis, dim in sides:
        size, length = (lax.axis_size(axis), shard.shape[dim])
        up = [(i, (i + 1) % size) for i in range(size - 1)]
        down = [(j, i) for i, j in up]
        last = lax.slice_in_dim(shard, length - width, length, axis=dim)
        first = lax.slice_in_dim(shard, 0, width, axis=dim)
        before = lax.ppermute(last, axis, up)
        after = lax.ppermute(first, axis, down)
        shard = jnp.concatenate([before, shard, after], axis=dim)
    return shard


def from_behind(block, axis, distance):
    devices = range(lax.axis_size(axis))
    route = [(i - distance, i) for i in devices if i - distance in devices]
    return lax.ppermute(block, axis, route)


def dft_blocks(length, sign):
    counter = jnp.arange(length, dtype=jnp.int32)
    turns = counter[:, None] * counter[None, :] % length
    angle = turns.astype(jnp.float32) * (2.0 * jnp.pi / length)
    norm_factor = 1.0 / jnp.sqrt(jnp.float32(length))
    cosine = jnp.cos(angle) * norm_factor
    sine = sign * jnp.sin(angle) * norm_factor
    return jnp.stack([jnp.stack([cosine, -sine]), jnp.stack([sine, cosine])])


def transform(image, sign):
    rows_here = image.shape[1]
    rows_all = rows_here * lax.axis_size("rows")
    first_row = lax.axis_index("rows") * rows_here
    across = jnp.einsum(
        "byix,oikx->byok", image, dft_blocks(image.shape[3], sign), precision=HIGHEST
    )
    table = dft_blocks(rows_all, sign)
    window = lax.dynamic_slice(
        table, (0, 0, 0, first_row), (2, 2, lax.axis_size("rows") * rows_here, rows_here)
    )
    return lax.psum_scatter(
        jnp.einsum("byix,oiky->kbox", across, window, precision=HIGHEST),
        "rows",
        scatter_dimension=0,
        tiled=True,
    ).transpose(1, 0, 2, 3)


def taps(widened, offset, frames, rows_here, columns):
    time_off = offset // 3
    row_off = offset % 3
    return jnp.concatenate(
        [
            widened[
                time_off : time_off + frames,
                row_off : row_off + rows_here,
                :,
                col_off : col_off + columns,
            ]
            for col_off in range(3)
        ],
        axis=2,
    )


def convolve(padded, kernel):
    frames = padded.shape[0] - 2
    rows_here = padded.shape[1] - 2
    width_in = padded.shape[2]
    columns = padded.shape[3]
    widened = jnp.pad(padded, ((0, 0), (0, 0), (0, 0), (1, 1)))
    blocks = kernel.reshape(9, 3 * width_in, kernel.shape[1])
    summed = jnp.zeros((frames, rows_here, kernel.shape[1], columns), jnp.float32)
    for offset in range(9):
        gathered = taps(widened, offset, frames, rows_here, columns)
        summed = summed + jnp.einsum(
            "tykx,kj->tyjx", gathered, blocks[offset], preferred_element_type=jnp.float32
        )
    return summed


def kernel_grad(padded, grad_out):
    frames, rows_here, columns = (grad_out.shape[0], grad_out.shape[1], grad_out.shape[3])
    widened = jnp.pad(padded, ((0, 0), (0, 0), (0, 0), (1, 1)))
    pieces = [
        jnp.einsum(
            "tykx,tyjx->kj",
            taps(widened, offset, frames, rows_here, columns),
            grad_out,
            preferred_element_type=jnp.float32,
        )
        for offset in range(9)
    ]
    return jnp.concatenate(pieces, axis=0)


def flipped(kernel):
    width_in = kernel.shape[0] // 27
    shaped = kernel.reshape(3, 3, 3, width_in, kernel.shape[1])[::-1, ::-1, ::-1]
    return shaped.transpose(0, 1, 2, 4, 3).reshape(27 * kernel.shape[1], width_in)


def activation_rim(values):
    return with_halo(values, (("frames", 0), ("rows", 1)), 1)


def gradient_rim(values):
    return with_halo(values, (("frames", 0), ("rows", 1)), 1)


def layer_forward(inputs, kernel, bias_row):
    padded = activation_rim(inputs)
    return (padded, convolve(padded, kernel) + bias_row.astype(jnp.float32)[None, None, :, None])


def layer_backward(padded, kernel, grad_hidden, needs_input):
    kernel_delta = kernel_grad(padded, grad_hidden)
    bias_delta = jnp.sum(grad_hidden, axis=(0, 1, 3), dtype=jnp.float32)
    input_delta = None
    if needs_input:
        input_delta = convolve(gradient_rim(grad_hidden), flipped(kernel))
    return (kernel_delta, bias_delta, input_delta)


def share(measured, sampled):
    frames = measured.shape[0]
    reach = (frames + 1) // frames
    before = []
    after = []
    for distance in range(1, reach + 1):
        for direction in (1, -1):
            moved = from_behind((measured, sampled), "frames", direction * distance)
            if direction == 1:
                before.insert(0, moved)
            else:
                after.append(moved)
    data_line = jnp.concatenate(
        [moved_pair[0] for moved_pair in before]
        + [measured]
        + [moved_pair[0] for moved_pair in after],
        axis=0,
    )
    mask_line = jnp.concatenate(
        [moved_pair[1] for moved_pair in before]
        + [sampled]
        + [moved_pair[1] for moved_pair in after],
        axis=0,
    )
    centre = reach * frames
    windows = []
    for radius in range(3):
        data_sum = data_line[centre - radius : centre - radius + frames]
        mask_sum = mask_line[centre - radius : centre - radius + frames]
        for offset in range(1 - radius, radius + 1):
            data_sum = data_sum + data_line[centre + offset : centre + offset + frames]
            mask_sum = mask_sum + mask_line[centre + offset : centre + offset + frames]
        windows.append(data_sum / jnp.maximum(mask_sum, 1.0)[:, :, None, None])
    return jnp.stack(windows, 1)


def adamw(weight, grad_piece, moment_one, moment_two):
    first_new = BETA_ONE * moment_one + (1.0 - BETA_ONE) * grad_piece
    second_new = BETA_TWO * moment_two + (1.0 - BETA_TWO) * grad_piece * grad_piece
    ascent = (
        first_new
        / (1.0 - BETA_ONE**STEP)
        / (jnp.sqrt(second_new / (1.0 - BETA_TWO**STEP)) + EPSILON)
    )
    weight_new = weight - RATE * (ascent + DECAY * weight)
    return (first_new, second_new, weight_new, weight_new.astype(jnp.bfloat16))


def local(
    kspace,
    line_mask,
    valid_flags,
    target,
    conv_in,
    conv_mid,
    conv_out,
    conv_bias,
    first_in,
    first_mid,
    first_out,
    first_bias,
    second_in,
    second_mid,
    second_out,
    second_bias,
):
    masters = (conv_in, conv_mid, conv_out, conv_bias)

    def reduce_grads(grads):
        shards = (
            lax.psum_scatter(
                grads[0].astype(jnp.bfloat16), "rows", scatter_dimension=2, tiled=True
            ).astype(jnp.float32),
            lax.psum_scatter(
                grads[1].astype(jnp.bfloat16), "rows", scatter_dimension=3, tiled=True
            ).astype(jnp.float32),
            lax.psum_scatter(
                grads[2].astype(jnp.bfloat16), "rows", scatter_dimension=2, tiled=True
            ).astype(jnp.float32),
            lax.psum_scatter(
                grads[3].astype(jnp.bfloat16), "rows", scatter_dimension=2, tiled=True
            ).astype(jnp.float32),
        )
        return lax.psum((shards[0], shards[1], shards[2], shards[3]), "frames")

    def micro_batch(carry, batch_data):
        grad_carry, loss_carry, count_carry = carry
        measured_full, mask_rows, frame_flags, wanted = batch_data
        full_in, full_mid, full_out, full_bias = (
            lax.all_gather(conv_in.astype(jnp.bfloat16), "rows", axis=2, tiled=True),
            lax.all_gather(conv_mid.astype(jnp.bfloat16), "rows", axis=3, tiled=True),
            lax.all_gather(conv_out.astype(jnp.bfloat16), "rows", axis=2, tiled=True),
            lax.all_gather(conv_bias.astype(jnp.bfloat16), "rows", axis=2, tiled=True),
        )
        sampled = mask_rows.astype(jnp.float32)
        measured = measured_full * sampled[:, :, None, None]
        shared = share(measured, sampled)
        frames, rows_here = (measured.shape[0], measured.shape[1])
        images = transform(shared.reshape(frames * 3, rows_here, 2, NX), 1.0).reshape(
            frames, 3, rows_here, 2, NX
        )
        shared_images = images.transpose(0, 2, 1, 3, 4).reshape(frames, rows_here, 6, NX)
        current = images[:, 0]
        unsampled = (1.0 - sampled)[:, :, None, None]
        no_bias = jnp.zeros((2,), jnp.bfloat16)

        def kernels_of(cascade):
            return [full_in[cascade]] + [full_mid[cascade, 0]] + [full_out[cascade].T]

        cascade = 0
        kernels = kernels_of(cascade)
        biases = [full_bias[cascade, layer_at] for layer_at in range(MIDS + 1)] + [no_bias]
        inputs = jnp.concatenate([current, shared_images], axis=2).astype(jnp.bfloat16)
        saved = []
        for layer_at in range(MIDS + 2):
            padded, hidden = layer_forward(inputs, kernels[layer_at], biases[layer_at])
            saved.append((padded, hidden))
            if layer_at < MIDS + 1:
                inputs = jax.nn.gelu(hidden).astype(jnp.bfloat16)
        current = transform(unsampled * transform(current + hidden, -1.0) + measured, 1.0)
        kept = [saved]
        frame_weight = frame_flags.astype(jnp.float32)[:, None, None, None]
        residual_error = current - wanted
        loss_part = jnp.sum(frame_weight * residual_error * residual_error)
        count_part = 2.0 * rows_here * NX * jnp.sum(frame_flags.astype(jnp.float32))
        grad_current = 2.0 * frame_weight * residual_error
        delta_in = [None] * CAS
        delta_mid = [None] * CAS
        delta_out = [None] * CAS
        delta_bias = [None] * CAS
        for cascade in reversed(range(CAS)):
            kernels = kernels_of(cascade)
            grad_sum = transform(unsampled * transform(grad_current, -1.0), 1.0)
            grad_hidden = grad_sum.astype(jnp.bfloat16)
            kernel_deltas = [None] * (MIDS + 2)
            bias_deltas = [None] * (MIDS + 2)
            grad_input = None
            for layer_at in reversed(range(MIDS + 2)):
                padded, hidden = kept[cascade][layer_at]
                if layer_at < MIDS + 1:
                    pullback = jax.vjp(jax.nn.gelu, hidden)[1]
                    grad_hidden = pullback(grad_input)[0].astype(jnp.bfloat16)
                needs_input = cascade > 0 or layer_at > 0
                kernel_deltas[layer_at], bias_deltas[layer_at], grad_input = layer_backward(
                    padded, kernels[layer_at], grad_hidden, needs_input
                )
            delta_in[cascade] = kernel_deltas[0]
            delta_mid[cascade] = jnp.stack(kernel_deltas[1 : MIDS + 1])
            delta_out[cascade] = kernel_deltas[MIDS + 1].T
            delta_bias[cascade] = jnp.stack(bias_deltas[0 : MIDS + 1])
        grads = (
            jnp.stack(delta_in),
            jnp.stack(delta_mid),
            jnp.stack(delta_out),
            jnp.stack(delta_bias),
        )
        grads = reduce_grads(grads)
        grad_carry = jax.tree.map(jnp.add, grad_carry, grads)
        return ((grad_carry, loss_carry + loss_part, count_carry + count_part), None)

    start_grads = jax.tree.map(jnp.zeros_like, masters)
    start = (start_grads, jnp.zeros((), jnp.float32), jnp.zeros((), jnp.float32))
    (summed, loss_local, count_local), unused = lax.scan(
        micro_batch, start, (kspace, line_mask, valid_flags, target)
    )
    summed = tuple(summed)
    loss_sum, valid_count = lax.psum((loss_local, count_local), ("frames", "rows"))
    divisor = jnp.maximum(valid_count, 1.0)
    grads = [grad_piece / divisor for grad_piece in summed]
    squares = sum((jnp.sum(grad_piece * grad_piece) for grad_piece in grads))
    grad_norm = jnp.sqrt(lax.psum(squares, "rows"))
    factor = jnp.minimum(1.0, CLIP / (grad_norm + 1e-06))
    firsts = (first_in, first_mid, first_out, first_bias)
    seconds = (second_in, second_mid, second_out, second_bias)
    results = [
        adamw(masters[which], grads[which] * factor, firsts[which], seconds[which])
        for which in range(4)
    ]
    return (
        loss_sum,
        valid_count,
        grad_norm,
        results[0][0],
        results[1][0],
        results[2][0],
        results[3][0],
        results[0][1],
        results[1][1],
        results[2][1],
        results[3][1],
        results[0][2],
        results[1][2],
        results[2][2],
        results[3][2],
        results[0][3],
        results[1][3],
        results[2][3],
        results[3][3],
    )


BF = jnp.bfloat16
F32 = jnp.float32
SQRT_TWO_OVER_PI = 0.7978845608028654
CUBIC = 0.044715 * SQRT_TWO_OVER_PI
UNITS = 16


def column_order():
    lanes = np.arange(128)
    return (lanes % 16) * 8 + lanes // 16


def dft_tables(sign):
    counter = np.arange(128)
    angle = (counter[:, None] * counter[None, :] % 128) * (2.0 * np.pi / 128)
    cosine, sine = np.cos(angle) / np.sqrt(128.0), sign * np.sin(angle) / np.sqrt(128.0)
    return np.stack([np.stack([cosine, -sine]), np.stack([sine, cosine])])


def make_tables():
    inverse, forward = dft_tables(1.0), dft_tables(-1.0)
    order = column_order()
    columns = inverse[:, :, :, order].transpose(1, 2, 0, 3).reshape(256, 256)
    blocks = np.arange(UNITS)[:, None] * 8

    def rows_of(first, kept):
        rows = blocks + first + np.arange(16)[None, :]
        inside = (rows >= 0) & (rows < 128) & (np.arange(16)[None, :] < kept)
        return np.clip(rows, 0, 127), inside

    rows, inside = rows_of(-3, 14)
    feature = inverse[:, :, rows, :] * inside[None, None, :, :, None]
    feature = feature.transpose(2, 3, 0, 1, 4).reshape(UNITS, 16, 2, 256)
    feature = np.tile(feature, (1, 1, 4, 1)).reshape(UNITS, 128, 256)
    to_lines = forward.reshape(2, 2, 128, UNITS, 8).transpose(0, 2, 3, 1, 4).reshape(256, 256)
    to_rows = inverse.transpose(0, 2, 1, 3).reshape(256, 256)
    lines_again = forward.transpose(0, 2, 1, 3).reshape(256, 256)
    rows, inside = rows_of(-2, 12)
    spread = inverse[:, :, rows, :] * inside[None, None, :, :, None]
    spread = spread.transpose(2, 0, 3, 1, 4).reshape(UNITS * 32, 256)
    permute = np.zeros((128, 128))
    permute[order, np.arange(128)] = 1.0
    pick_out = np.zeros((64, 10, 256))
    pick_back = np.zeros((10, 288, 64))
    for time_off in range(3):
        for row_off in range(3):
            for col_off in range(3):
                tap = (time_off * 3 + row_off) * 3 + col_off
                for part in range(2):
                    for row in range(8):
                        lane = (time_off * 3 + col_off) * 16 + part * 8 + row
                        pick_out[tap * 2 + part, row + row_off, lane] = 1.0
                    for row in range(12):
                        into = row + row_off - 2
                        if 0 <= into < 10:
                            at = (time_off * 3 + col_off) * 32 + part * 16 + row
                            pick_back[into, at, tap * 2 + part] = 1.0
    made = dict(
        columns=columns,
        feature=feature,
        to_lines=to_lines,
        lines_again=lines_again,
        to_rows=to_rows,
        spread=spread,
        permute=permute,
        pick_out=pick_out.reshape(64, 2560),
        pick_back=pick_back.reshape(2880, 64),
    )
    return {name: jnp.asarray(table.astype(ml_dtypes.bfloat16)) for name, table in made.items()}


def dot(left, right):
    return jnp.dot(left, right, preferred_element_type=F32)


def dot_first(left, right):
    return lax.dot_general(left, right, (((0,), (0,)), ((), ())), preferred_element_type=F32)


def next_column(values):
    lane = lax.broadcasted_iota(jnp.int32, values.shape, 1)
    inner = pltpu.roll(values, 112, 1)
    wrapped = jnp.where(lane == 127, 0.0, pltpu.roll(values, 111, 1))
    return jnp.where(lane < 112, inner, wrapped)


def previous_column(values):
    lane = lax.broadcasted_iota(jnp.int32, values.shape, 1)
    inner = pltpu.roll(values, 16, 1)
    wrapped = jnp.where(lane == 0, 0.0, pltpu.roll(values, 17, 1))
    return jnp.where(lane >= 16, inner, wrapped)


def put_slabs(store, values):
    store(slice(1, 9), values.astype(BF).reshape(8, 16, 128))
    first, last = values[0:16], values[112:128]
    at = lax.broadcasted_iota(jnp.int32, (16, 128), 0)
    before = jnp.where(at == 0, 0.0, pltpu.roll(last, 1, 0))
    after = jnp.where(at == 15, 0.0, pltpu.roll(first, 15, 0))
    store(slice(0, 1), before.astype(BF).reshape(1, 16, 128))
    store(slice(9, 10), after.astype(BF).reshape(1, 16, 128))


def two_rows(ref, frame, pair, count, first_slab):
    upper = ref[frame, pair : pair + count, first_slab : first_slab + 8]
    lower = ref[frame, pair + 1 : pair + 1 + count, first_slab : first_slab + 8]
    rows = count * 128
    return jnp.concatenate([upper.reshape(rows, 128), lower.reshape(rows, 128)], axis=1)


def gelu_and_slope(hidden):
    square = hidden * hidden
    half = 0.5 * jnp.tanh(hidden * (CUBIC * square + SQRT_TWO_OVER_PI)) + 0.5
    active = hidden * half
    slope = half + active * (1.0 - half) * (6.0 * CUBIC * square + 2.0 * SQRT_TWO_OVER_PI)
    return active, slope


def place():
    return tuple(lax.axis_index(name) for name in ("frames", "half", "chip", "core"))


def lines_kernel(
    valid, kspace, line_mask, target, columns_table, permute, conv_mid, conv_in, conv_out, conv_bias,
    beside, other, far, mine_target, both, images, tiles,
):
    f, half, chip, core = place()
    quarter = chip * 2 + core
    sampled = line_mask[...].astype(F32)
    wide = jnp.concatenate([sampled, jnp.zeros((8, 112), F32)], axis=1)
    column = jnp.transpose(jnp.concatenate([wide, jnp.zeros((120, 128), F32)], axis=0))
    placed = pltpu.roll(wide, (half * 4 + quarter) * 16, 1)
    total = jnp.zeros((1, 128), F32)
    flags = []
    for batch in range(2):
        for frame in range(4):
            flag = jnp.zeros((1, 128), F32) + valid[batch, frame].astype(F32)
            flags.append(flag)
            total = total + flag
    for batch in range(2):
        shown = [[], []]
        sampled_lines = []
        for frame in range(4):
            at = batch * 4 + frame
            own = column[0:16, at : at + 1]
            lines = [kspace[batch, frame, pl.ds(part, 16, stride=2), :] * own for part in range(2)]
            sampled_lines.append(jnp.concatenate(lines, axis=1).astype(BF))
            for part in range(2):
                shown[part].append(target[batch, frame, pl.ds(part, 16, stride=2), :])
        both[batch, 0:64] = dot(jnp.concatenate(sampled_lines, axis=0), columns_table[...]).astype(BF)
        rows = [placed[batch * 4 : batch * 4 + 4]] + flags[batch * 4 : batch * 4 + 4] + [total, jnp.zeros((7, 128), F32)]
        both[batch, 64:80, 0:128] = jnp.concatenate(rows, axis=0).astype(BF)
        both[batch, 64:80, 128:256] = jnp.zeros((16, 128), BF)
        for part in range(2):
            image = jnp.concatenate(shown[part], axis=0).astype(BF)
            image = dot(image, permute[...]).astype(BF)
            for frame in range(4):
                images[batch, frame, :, part * 128 : part * 128 + 128] = image[frame * 16 : frame * 16 + 16]
    for step, to in ((1, beside), (2, other), (3, far)):
        batch = half if step == 1 else 1 - half
        to[0:80] = both[batch]
        for sibling in range(2):
            frame = jnp.bitwise_xor(quarter, (step % 2) * 2 + sibling)
            to[144 + sibling * 16 : 160 + sibling * 16] = images[batch, frame]
    for sibling in range(2):
        mine_target[sibling * 16 : sibling * 16 + 16] = images[half, jnp.bitwise_xor(quarter, sibling)]
    tiles[...] = jnp.zeros_like(tiles)
    for tile in range(13):
        tiles[tile] = conv_mid[:, tile * 128 : tile * 128 + 128]
    tiles[13, :, 0:64] = conv_mid[:, 1664:1728]
    for part in range(2):
        for piece in range(4):
            row = part * 4 + piece
            tiles[13, row : row + 1, 64:118] = conv_out[part : part + 1, piece * 54 : piece * 54 + 54]
    tiles[14] = conv_in[:, 0:128]
    tiles[15, :, 0:88] = conv_in[:, 128:216]
    wide = jnp.concatenate([conv_bias[...], jnp.zeros((2, 120), F32)], axis=1)
    wide = jnp.transpose(jnp.concatenate([wide, jnp.zeros((126, 128), F32)], axis=0))
    tiles[15, :, 88:90] = wide[0:8, 0:2]
    packed = tiles[...].reshape(128, 128).astype(BF)
    packed = jnp.concatenate([packed[0:64], packed[64:128]], axis=1)
    for to in (beside, other, far):
        to[80:144] = packed


def unpack_weights(own, other, whole):
    f, half, chip, core = place()
    for side, source in enumerate((own, other)):
        for slot in range(4):
            row = jnp.bitwise_xor(half * 4 + chip * 2 + core, slot * 2 + side)
            row = pl.multiple_of(row * 8, 8)
            values = source[slot * 64 : slot * 64 + 64].astype(F32)
            for part in range(2):
                half_of = values[:, part * 128 : part * 128 + 128].reshape(8, 8, 128)
                whole[part * 8 : part * 8 + 8, pl.ds(row, 8), :] = half_of


def unpack_last(whole, line, taps):
    for owner in range(8):
        for part in range(2):
            for piece in range(4):
                at = owner * 216 + piece * 54
                row = owner * 8 + part * 4 + piece
                line[part : part + 1, at : at + 54] = whole[13, row : row + 1, 64:118]
    taps[...] = jnp.zeros_like(taps)
    for tap in range(27):
        for part in range(2):
            row = tap * 2 + part
            taps[row : row + 1, 0:64] = line[part : part + 1, tap * 64 : tap * 64 + 64]
    return taps[...].astype(BF)[:, 0:64]


def forward_weight_kernel(own, other, pick_out, fwd_in, fwd_mid, fwd_out, bias, whole, line, taps):
    unpack_weights(own, other, whole)
    zero = jnp.zeros((64, 64), F32)
    turned = [jnp.transpose(whole[tile]) for tile in range(16)]

    def of_tap(time_off, row_off, col_off):
        tap = (time_off * 3 + row_off) * 3 + col_off
        return turned[tap // 2][(tap % 2) * 64 : (tap % 2) * 64 + 64]

    for time_off in range(4):
        for col_off in range(3):
            at = (time_off * 3 + col_off) * 256
            if time_off == 0:
                fwd_mid[at : at + 256, 128:256] = jnp.zeros((256, 128), BF)
            if time_off == 3:
                fwd_mid[at : at + 256, 0:128] = jnp.zeros((256, 128), BF)
    for time_off in range(3):
        for col_off in range(3):
            for level in range(4):
                left = of_tap(time_off, level, col_off) if level < 3 else zero
                right = of_tap(time_off, level - 1, col_off) if level > 0 else zero
                strip = jnp.concatenate([left, right], axis=1).astype(BF)
                for pair in range(2):
                    at = ((time_off + pair) * 3 + col_off) * 256 + level * 64
                    fwd_mid[at : at + 64, pair * 128 : pair * 128 + 128] = strip
    first = jnp.concatenate([turned[14], turned[15]], axis=0)
    fwd_in[...] = jnp.zeros_like(fwd_in)
    pad = jnp.zeros((8, 64), F32)
    for time_off in range(3):
        for col_off in range(3):
            three = []
            for row_off in range(3):
                tap = (time_off * 3 + row_off) * 3 + col_off
                three.append(first[tap * 8 : tap * 8 + 8, 0:64])
            left = jnp.concatenate(three + [pad], axis=0)
            right = jnp.concatenate([pad] + three, axis=0)
            strip = jnp.concatenate([left, right], axis=1).astype(BF)
            at = (time_off * 3 + col_off) * 128
            for pair in range(6):
                fwd_in[at + pair * 16 : at + pair * 16 + 32, pair * 128 : pair * 128 + 128] = strip
    bias[...] = jnp.zeros_like(bias)
    for layer in range(2):
        row = turned[15][88 + layer : 89 + layer, 0:64]
        row = jnp.concatenate([row, row], axis=1)
        for pair in range(6):
            bias[layer : layer + 1, pair * 128 : pair * 128 + 128] = row
    spread = dot_first(unpack_last(whole, line, taps), pick_out[...]).astype(BF)
    for row in range(10):
        fwd_out[row * 64 : row * 64 + 64, :] = spread[:, row * 256 : row * 256 + 256]


def backward_weight_kernel(own, other, pick_back, bwd_mid, bwd_out, whole, line, taps):
    unpack_weights(own, other, whole)
    zero = jnp.zeros((64, 64), F32)
    plain = [whole[tile] for tile in range(14)]

    def of_tap(time_off, row_off, col_off):
        tap = (time_off * 3 + row_off) * 3 + col_off
        return plain[tap // 2][:, (tap % 2) * 64 : (tap % 2) * 64 + 64]

    for time_off in range(4):
        for col_off in range(3):
            at = (time_off * 3 + col_off) * 256
            if time_off == 0:
                bwd_mid[at : at + 256, 128:256] = jnp.zeros((256, 128), BF)
            if time_off == 3:
                bwd_mid[at : at + 256, 0:128] = jnp.zeros((256, 128), BF)
    for time_off in range(3):
        for col_off in range(3):
            for level in range(4):
                left = of_tap(time_off, 2 - level, col_off) if level < 3 else zero
                right = of_tap(time_off, 3 - level, col_off) if level > 0 else zero
                strip = jnp.concatenate([left, right], axis=1).astype(BF)
                for pair in range(2):
                    at = ((2 + pair - time_off) * 3 + 2 - col_off) * 256 + level * 64
                    bwd_mid[at : at + 64, pair * 128 : pair * 128 + 128] = strip
    back = dot(pick_back[...], unpack_last(whole, line, taps)).astype(BF)
    for pair in range(5):
        at = pair * 2 * 288
        bwd_out[:, pair * 128 : pair * 128 + 128] = jnp.concatenate(
            [back[at : at + 288], back[at + 288 : at + 576]], axis=1
        )


def move(source, target, semaphores, at):
    copy = pltpu.make_async_copy(source, target, semaphores.at[at])
    copy.start()
    return copy


def forward_kernel(*refs):
    gathered, refs = refs[0:8], refs[8:]
    row_tables, fwd_in_hbm, fwd_mid_hbm, fwd_out, bias = refs[0:5]
    branch, stats, lines, natural, turned, active_out, slope_in, slope_out = refs[5:13]
    rows_table, fwd_in, fwd_mid, came = refs[13:17]
    spectrum, masks, seen, feature, active, hidden, hidden_other, second, second_other, taps = refs[17:]
    f, half, chip, core = place()
    quarter = chip * 2 + core
    block = f * 4 + quarter
    loads = [move(row_tables.at[block], rows_table, came, 0), move(fwd_in_hbm, fwd_in, came, 1)]
    spectrum[0:2] = jnp.zeros((2, 128, 256), BF)
    spectrum[18:20] = jnp.zeros((2, 128, 256), BF)
    feature[0] = jnp.zeros((10, 16, 128), BF)
    feature[17] = jnp.zeros((10, 16, 128), BF)
    active[0] = jnp.zeros((6, 10, 16, 128), BF)
    active[17] = jnp.zeros((6, 10, 16, 128), BF)
    turned[0] = jnp.zeros((128, 512), BF)
    turned[17] = jnp.zeros((128, 512), BF)
    taps[0] = jnp.zeros((144, 128), F32)
    taps[17] = jnp.zeros((144, 128), F32)
    total = jnp.zeros((1, 128), F32)
    masks[...] = jnp.zeros_like(masks)
    for at in range(8):
        side, which = at // 4, at % 4
        group = jnp.bitwise_xor(f, which)
        for chips_away in range(4):
            row = jnp.bitwise_xor(half * 4 + quarter, chips_away * 2 + side) * 16
            row = pl.multiple_of(row, 16)
            for frame in range(4):
                at_row = chips_away * 64 + frame * 16
                spectrum[2 + group * 4 + frame, pl.ds(row, 16), :] = gathered[at][at_row : at_row + 16]
        flags = gathered[at][256:272, 0:128].astype(F32)
        if side == 0:
            total = total + 0.25 * flags[8:9]
            masks[group] = masks[group] + flags[0:8]
        else:
            masks[group, 0:4] = masks[group, 0:4] + flags[0:4]
    seen[...] = jnp.zeros_like(seen)
    for group in range(4):
        seen[2 + group * 4 : 6 + group * 4] = masks[group, 0:4]
    stats[...] = jnp.zeros_like(stats)
    for part in range(2):
        stats[0:1, part * 128 : part * 128 + 128] = 1.0 - masks[f, pl.ds(quarter, 1), :]
    stats[1:2, 0:128] = total
    stats[2:3, 0:128] = 0.25 * masks[f, pl.ds(4 + quarter, 1), :]
    mine = spectrum[2 + block]
    lines[0:128] = mine[:, 0:128]
    lines[128:256] = mine[:, 128:256]
    sampled = seen[0:20]
    reach = [sampled[2:18]]
    reach.append(sampled[1:17] + sampled[2:18] + sampled[3:19])
    reach.append(reach[1] + sampled[0:16] + sampled[4:20])
    scales = [1.0 / jnp.maximum(count, 1.0) for count in reach]
    scales = [jnp.concatenate([scale, scale], axis=1) for scale in scales]

    loads[0].wait()
    channel = lax.rem(lax.broadcasted_iota(jnp.int32, (128, 256), 0), 8)
    table = rows_table[...].astype(F32)
    tables = [
        jnp.where(channel < 4, table, 0.0),
        jnp.where((channel == 4) | (channel == 5), table, 0.0),
        jnp.where(channel > 5, table, 0.0),
    ]
    for frame in range(16):
        near = [spectrum[frame + step].astype(F32) for step in range(5)]
        sums = [near[2]]
        sums.append(near[1] + near[2] + near[3])
        sums.append(sums[1] + near[0] + near[4])
        left = [(tables[radius] * scales[radius][frame : frame + 1]).astype(BF) for radius in range(3)]
        right = []
        for radius in range(3):
            value = sums[radius].astype(BF)
            right += [value[:, 0:128], value[:, 128:256]]
        image = dot(jnp.concatenate(left, axis=1), jnp.concatenate(right, axis=0))
        natural[frame] = image.astype(BF)

        def store(slabs, values, frame=frame):
            feature[frame + 1, slabs] = values

        put_slabs(store, jnp.transpose(image.astype(BF)).astype(F32))
    loads.append(move(fwd_mid_hbm, fwd_mid, came, 2))
    loads[1].wait()
    half_lane = lax.broadcasted_iota(jnp.int32, (1, 128), 1) // 64

    def finish_first(hidden, frame, pair, at):
        chunk = hidden[at : at + 128, pair * 128 : pair * 128 + 128]
        value, slope = gelu_and_slope(chunk + bias[0:1, pair * 128 : pair * 128 + 128])
        if pair in (0, 5):
            row = block * 8 - 2 + 2 * pair + half_lane
            value = jnp.where((row >= 0) & (row < 128), value, 0.0)
        else:
            at = (pair - 1) * 128
            slope_in[pl.ds(frame * 128, 128), at : at + 128] = slope.astype(BF)
            turned[frame + 1, :, at : at + 128] = jnp.transpose(value.astype(BF))

        def store(slabs, values):
            active[frame + 1, pair, slabs] = values

        put_slabs(store, value)

    def first_product(group):
        pieces = []
        for time_off in range(3):
            for col_off in range(3):
                piece = feature[group * 2 + time_off : group * 2 + time_off + 2, col_off : col_off + 8]
                pieces.append(piece.reshape(256, 128))
        return dot(jnp.concatenate(pieces, axis=1), fwd_in[...])

    def finish_frames(hidden, group):
        for step in range(2):
            for pair in range(6):
                finish_first(hidden, group * 2 + step, pair, step * 128)

    firsts = (hidden, hidden_other)
    hidden[...] = first_product(0)
    for group in range(1, 8):
        firsts[group % 2][...] = first_product(group)
        finish_frames(firsts[(group - 1) % 2], group - 1)
    finish_frames(firsts[1], 7)
    loads[2].wait()

    def finish_second(second, pair_of, pair, at):
        for side in range(2):
            chunk = second[at : at + 128, side * 128 : side * 128 + 128]
            value, slope = gelu_and_slope(chunk + bias[1:2, 0:128])
            if pair in (0, 4):
                row = block * 8 - 1 + 2 * pair + half_lane
                inside = (row >= 0) & (row < 128)
                value = jnp.where(inside, value, 0.0)
                slope = jnp.where(inside, slope, 0.0)
            row = (pair_of * 2 + side) * 128
            active_out[pl.ds(row, 128), pair * 128 : pair * 128 + 128] = value.astype(BF)
            slope_out[pl.ds(row, 128), pair * 128 : pair * 128 + 128] = slope.astype(BF)

    def finish_group(second, group):
        for pair in range(5):
            finish_second(second, group, pair, pair * 128)
        rows = pl.ds(group * 256, 256)
        made = dot(active_out[rows], fwd_out[...])
        for frame in range(2):
            taps[group * 2 + frame + 1] = jnp.transpose(made[frame * 128 : frame * 128 + 128])[0:144]

    def second_product(pair_of):
        pieces = []
        for step in range(4):
            for col_off in range(3):
                pieces.append(two_rows(active, pair_of * 2 + step, 0, 5, col_off))
        return dot(jnp.concatenate(pieces, axis=1), fwd_mid[...])

    seconds = (second, second_other)
    second[...] = second_product(0)
    for group in range(1, 8):
        seconds[group % 2][...] = second_product(group)
        finish_group(seconds[(group - 1) % 2], group - 1)
    finish_group(seconds[1], 7)
    for frame in range(16):
        columns = []
        for col_off in range(3):
            value = None
            for time_off in range(3):
                at = (time_off * 3 + col_off) * 16
                piece = taps[frame + time_off, at : at + 16]
                value = piece if value is None else value + piece
            columns.append(value)
        result = previous_column(columns[0]) + columns[1] + next_column(columns[2])
        branch[frame * 16 : frame * 16 + 16] = result.astype(BF)


def consistency_kernel(
    gathered, lines, stats, mine_target, beside, other, far, others, to_lines, to_rows, lines_again, spread, out, loss, target
):
    f, half, chip, core = place()
    for slot, source in enumerate((mine_target, beside, other, far)):
        at = 144 if slot else 0
        for side, image in enumerate((source[at : at + 16], others[256 + slot * 16 : 272 + slot * 16])):
            row = jnp.bitwise_xor(half * 4 + chip * 2 + core, slot * 2 + side) * 16
            row = pl.multiple_of(row, 16)
            for part in range(2):
                target[pl.ds(part * 128 + row, 16), :] = image[:, part * 128 : part * 128 + 128]
    weight = stats[2:3, 0:128]
    free = jnp.transpose(jnp.zeros((128, 128), F32) + stats[0:1, 0:128])
    free = jnp.concatenate([free, free], axis=0)
    wanted = target[...]
    made = dot(to_lines[...], gathered[...])
    wanted_spectrum = dot(lines_again[...], wanted)
    held = lines[...].astype(F32)
    kept = free * (made + held) + held
    grad = (free * (kept - wanted_spectrum) * (2.0 * weight)).astype(BF)
    out[...] = dot(spread[...], grad).astype(BF)
    residual = dot(to_rows[...], kept.astype(BF)) - wanted.astype(F32)
    loss[...] = jnp.zeros((8, 128), F32) + jnp.sum(residual * residual * weight)


def backward_kernel(
    grads, bwd_out_hbm, slope_out, active, turned, bwd_mid_hbm, slope_in, natural,
    out,
    bwd_out, bwd_mid, came,
    stack, product, product_other, grad_mid, grad_in, result, result_other, sum_mid, sum_out, sum_in, patches, tall, tiles, line,
):
    loads = [move(bwd_out_hbm, bwd_out, came, 0), move(bwd_mid_hbm, bwd_mid, came, 1)]
    zero32 = jnp.zeros((96, 128), BF)
    stack[0:96, 1920:2048] = zero32
    stack[192:288, 0:128] = zero32
    for frame in range(16):
        value = grads[frame * 32 : frame * 32 + 32].astype(F32)
        shifted = [next_column(value).astype(BF), value.astype(BF), previous_column(value).astype(BF)]
        for time_off in range(3):
            to = frame + time_off - 1
            if 0 <= to < 16:
                for col_off in range(3):
                    at = (time_off * 3 + col_off) * 32
                    stack[at : at + 32, to * 128 : to * 128 + 128] = shifted[col_off]
    grad_mid[0] = jnp.zeros((5, 10, 16, 128), BF)
    grad_mid[17] = jnp.zeros((5, 10, 16, 128), BF)
    tall[...] = jnp.zeros_like(tall)

    lane = lax.broadcasted_iota(jnp.int32, (1, 128), 1)
    bias_mid = jnp.zeros((1, 128), F32)
    buffers = (product, product_other)

    def finish_mid(buffer, group):
        own = jnp.zeros((1, 128), F32)
        for step in range(4):
            frame = group * 4 + step
            for pair in range(5):
                chunk = buffer[step * 128 : step * 128 + 128, pair * 128 : pair * 128 + 128]
                slope = slope_out[frame * 128 : frame * 128 + 128, pair * 128 : pair * 128 + 128]
                value = (chunk * slope.astype(F32)).astype(BF).astype(F32)
                added = jnp.sum(value, axis=0, keepdims=True)
                if pair == 0:
                    added = jnp.where(lane >= 64, added, 0.0)
                if pair == 4:
                    added = jnp.where(lane < 64, added, 0.0)
                own = own + added

                def store(slabs, values, frame=frame, pair=pair):
                    grad_mid[frame + 1, pair, slabs] = values

                put_slabs(store, value)
        return own

    loads[0].wait()
    groups = 16 // 4
    for group in range(groups + 1):
        if group < groups:
            at = group * 4 * 128
            buffers[group % 2][...] = dot_first(stack[:, at : at + 4 * 128], bwd_out[...])
        if group > 0:
            bias_mid = bias_mid + finish_mid(buffers[(group - 1) % 2], group - 1)

    made = dot(stack[...], active[...])
    for pair in range(5):
        sum_out[pair] = made[:, pair * 128 : pair * 128 + 128]
    for group in range(16 // 4):
        frames = [group * 4 + step for step in range(4)]
        left = jnp.concatenate([turned[frame : frame + 3].reshape(384, 512) for frame in frames], axis=1)
        right = []
        for col_off in range(3):
            right.append(jnp.concatenate([two_rows(grad_mid, frame + 1, 0, 4, 2 - col_off) for frame in frames], axis=0))
        made = dot(left, jnp.concatenate(right, axis=1))
        sum_mid[...] = made if group == 0 else sum_mid[...] + made

    def lay_out_mid(time_off, row_off):
        for col_off in range(3):
            tap = (time_off * 3 + row_off) * 3 + col_off
            at, lane = time_off * 128, col_off * 256
            upper = sum_mid[at : at + 64, lane + (2 - row_off) * 64 : lane + (2 - row_off) * 64 + 64]
            lower = sum_mid[at + 64 : at + 128, lane + (3 - row_off) * 64 : lane + (3 - row_off) * 64 + 64]
            tall[tap * 64 : tap * 64 + 64, 0:64] = upper + lower

    def lay_out_last():
        for row_off in range(3):
            value = None
            for row in range(2, 10):
                lane = (row - 2 + row_off) * 64
                piece = sum_out[lane // 128, pl.ds(row, 18, stride=16), :][:, lane % 128 : lane % 128 + 64]
                value = piece if value is None else value + piece
            for time_off in range(3):
                for col_off in range(3):
                    tap = (time_off * 3 + row_off) * 3 + col_off
                    for part in range(2):
                        row = (time_off * 3 + col_off) * 2 + part
                        line[part : part + 1, tap * 64 : tap * 64 + 64] = value[row : row + 1]

    def lay_out_pieces():
        for owner in range(8):
            for part in range(2):
                for piece in range(4):
                    at = owner * 216 + piece * 54
                    row = owner * 8 + part * 4 + piece
                    tiles[13, row : row + 1, 64:118] = line[part : part + 1, at : at + 54]

    def lay_out_patches(first, last):
        for frame in range(first, last):
            value = natural[frame].astype(F32)
            shifted = (previous_column(value).astype(BF), natural[frame], next_column(value).astype(BF))
            for col_off in range(3):
                for pair in range(4):
                    piece = shifted[col_off][pair * 16 + 16 : pair * 16 + 48]
                    for time_off in range(3):
                        to = frame - time_off + 1
                        if 0 <= to < 16:
                            at = (time_off * 3 + col_off) * 32
                            lane = (to * 4 + pair) * 128
                            patches[at : at + 32, lane : lane + 128] = piece

    def input_product(group):
        rows = []
        for half_of in range(2):
            pieces = []
            for step in range(4):
                for col_off in range(3):
                    pieces.append(two_rows(grad_mid, group * 4 + half_of * 2 + step, 0, 4, col_off))
            rows.append(jnp.concatenate(pieces, axis=1))
        return dot(jnp.concatenate(rows, axis=0), bwd_mid[...])

    def finish_input(buffer, group):
        own = jnp.zeros((1, 128), F32)
        for half_of in range(2):
            for pair in range(4):
                for side in range(2):
                    frame = group * 4 + half_of * 2 + side
                    at = half_of * 512 + pair * 128
                    chunk = buffer[at : at + 128, side * 128 : side * 128 + 128]
                    slope = slope_in[frame * 128 : frame * 128 + 128, pair * 128 : pair * 128 + 128]
                    value = (chunk * slope.astype(F32)).astype(BF)
                    grad_in[frame * 512 + pair * 128 : frame * 512 + pair * 128 + 128, :] = value
                    own = own + jnp.sum(value.astype(F32), axis=0, keepdims=True)
        return own

    loads[1].wait()
    patches[0:96, 0:512] = jnp.zeros((96, 512), BF)
    patches[192:288, 7680:8192] = jnp.zeros((96, 512), BF)
    results = (result, result_other)
    bias_in = jnp.zeros((1, 128), F32)
    for group in range(5):
        if group < 4:
            results[group % 2][...] = input_product(group)
        if group == 0:
            for time_off in range(3):
                lay_out_mid(time_off, 0)
            lay_out_last()
            lay_out_patches(0, 4)
        else:
            bias_in = bias_in + finish_input(results[(group - 1) % 2], group - 1)
        if group == 1:
            for time_off in range(3):
                lay_out_mid(time_off, 1)
            lay_out_patches(4, 10)
        if group == 2:
            for time_off in range(3):
                lay_out_mid(time_off, 2)
            lay_out_patches(10, 16)
        if group == 3:
            for tile in range(14):
                tiles[tile] = jnp.transpose(tall[tile * 128 : tile * 128 + 128])[0:64]
            lay_out_pieces()

    sum_in[...] = dot(patches[...], grad_in[...])
    for time_off in range(3):
        for row_off in range(3):
            for col_off in range(3):
                tap = (time_off * 3 + row_off) * 3 + col_off
                at = (time_off * 3 + col_off) * 32 + row_off * 8
                upper = sum_in[at : at + 8, 0:64]
                lower = sum_in[at + 8 : at + 16, 64:128]
                tall[1792 + tap * 8 : 1792 + tap * 8 + 8, 0:64] = upper + lower
    tall[2008:2009, 0:64] = bias_in[:, 0:64] + bias_in[:, 64:128]
    tall[2009:2010, 0:64] = bias_mid[:, 0:64] + bias_mid[:, 64:128]
    for tile in range(14, 16):
        tiles[tile] = jnp.transpose(tall[tile * 128 : tile * 128 + 128])[0:64]
    for quarter in range(4):
        for owner in range(8):
            value = tiles[quarter * 4 : quarter * 4 + 4, owner * 8 : owner * 8 + 8]
            out[quarter * 8 + owner] = value.reshape(32, 128).astype(BF)


def sum_kernel(parts, stats, loss, shard, shared):
    total = parts[0].astype(F32)
    for source in range(1, 32):
        total = total + parts[source].astype(F32)
    divisor = jnp.maximum(stats[1:2, 0:1] * (2.0 * 128 * 128), 1.0)
    total = total / divisor
    shard[...] = total
    lane = lax.broadcasted_iota(jnp.int32, (32, 128), 1)
    shared[...] = jnp.where(lane == 0, jnp.sum(total * total), loss[0:1] + jnp.zeros((32, 128), F32))


def update_kernel(
    own, near, mid, far, messages, stats,
    w_in, w_mid, w_out, w_bias, f_in, f_mid, f_out, f_bias, s_in, s_mid, s_out, s_bias,
    loss_sum, valid_count, grad_norm, mf_in, mf_mid, mf_out, mf_bias, ms_in, ms_mid, ms_out, ms_bias,
    mw_in, mw_mid, mw_out, mw_bias, mc_in, mc_mid, mc_out, mc_bias,
    shards, g_mid, g_in, g_out, g_bias,
):
    f, half, chip, core = place()
    for slot, source in enumerate((own, near, mid, far)):
        shards[jnp.bitwise_xor(f, slot)] = source[...]
    message = jnp.sum(messages[...], axis=0, keepdims=True)
    norm = jnp.sqrt(message[:, 0:1])
    loss_sum[0, 0] = jnp.sum(message[:, 1:2])
    valid_count[0, 0] = jnp.sum(stats[1:2, 0:1]) * (2.0 * 128 * 128)
    grad_norm[0, 0] = jnp.sum(norm)
    factor = jnp.minimum(1.0, CLIP / (norm + 1e-06))

    def tile_of(tile):
        at = (tile % 4) * 8
        return shards[tile // 4, at : at + 8]

    for tile in range(13):
        g_mid[:, tile * 128 : tile * 128 + 128] = tile_of(tile)
    mixed = tile_of(13)
    g_mid[:, 1664:1728] = mixed[:, 0:64]
    for part in range(2):
        for piece in range(4):
            row = part * 4 + piece
            g_out[part : part + 1, piece * 54 : piece * 54 + 54] = mixed[row : row + 1, 64:118]
    g_in[:, 0:128] = tile_of(14)
    mixed = tile_of(15)
    g_in[:, 128:216] = mixed[:, 0:88]
    square = jnp.concatenate([mixed, jnp.zeros((120, 128), F32)], axis=0)
    g_bias[...] = jnp.transpose(square)[88:90, 0:8]
    for grad, weight, one, two, new_one, new_two, new_weight, new_copy in (
        (g_in, w_in, f_in, s_in, mf_in, ms_in, mw_in, mc_in),
        (g_mid, w_mid, f_mid, s_mid, mf_mid, ms_mid, mw_mid, mc_mid),
        (g_out, w_out, f_out, s_out, mf_out, ms_out, mw_out, mc_out),
        (g_bias, w_bias, f_bias, s_bias, mf_bias, ms_bias, mw_bias, mc_bias),
    ):
        results = adamw(weight[...], grad[...] * factor, one[...], two[...])
        for ref, value in zip((new_one, new_two, new_weight, new_copy), results):
            ref[...] = value


VECTOR = pl.BlockSpec(memory_space=pltpu.VMEM)
SCALAR = pl.BlockSpec(memory_space=pltpu.SMEM)
LEFT = pl.BlockSpec(memory_space=pl.ANY)


def near(value):
    return pltpu.with_memory_space_constraint(value, pltpu.VMEM)


def shape(*dims, dtype=BF):
    return jax.ShapeDtypeStruct(dims, dtype)


def kernel_call(kernel, name, micros, megabytes, operands, results, scratch, in_specs=None, out_specs=None):
    return pl.pallas_call(
        kernel,
        name=name,
        out_shape=results,
        in_specs=in_specs or [VECTOR] * len(operands),
        out_specs=out_specs or [VECTOR] * len(results),
        scratch_shapes=scratch,
        cost_estimate=pl.CostEstimate(flops=int(micros * 1e9), bytes_accessed=0, transcendentals=0),
        compiler_params=pltpu.CompilerParams(vmem_limit_bytes=megabytes * 2**20),
    )(*operands)


def swap(value, axis, bit):
    return lax.ppermute(value, axis, [(i, i ^ bit) for i in range(lax.axis_size(axis))])


def by_rows(
    kspace, line_mask, valid_flags, target, conv_in, conv_mid, conv_out, conv_bias,
    first_in, first_mid, first_out, first_bias, second_in, second_mid, second_out, second_bias,
):
    tables = make_tables()

    mine, theirs, far, mine_target = kernel_call(
        lines_kernel,
        "prepare_lines",
        2,
        56,
        [
            valid_flags, kspace.reshape(2, 4, 32, 128), line_mask.reshape(8, 16), target.reshape(2, 4, 32, 128),
            tables["columns"], tables["permute"], conv_mid[0, 0].T, conv_in[0].T, conv_out[0], conv_bias[0],
        ],
        [shape(176, 256), shape(176, 256), shape(176, 256), shape(32, 256)],
        [pltpu.VMEM((2, 80, 256), BF), pltpu.VMEM((2, 4, 16, 256), BF), pltpu.VMEM((16, 8, 128), F32)],
        in_specs=[SCALAR] + [VECTOR] * 9,
    )

    sent = ((mine, 1), (theirs, 2), (far, 3))
    beside, other, far = (swap(value, ("half", "chip"), step) for value, step in sent)

    sources = (mine, beside, other, far)
    flags = mine[64:80] + beside[64:80] + other[64:80] + far[64:80]
    column = jnp.concatenate([source[0:64] for source in sources] + [flags], axis=0)
    gathered = [column] + [swap(column, "frames", step) for step in (1, 2, 3)]
    images = [mine_target, beside[144:176], other[144:176], far[144:176]]
    chips = jnp.concatenate([source[80:144] for source in sources] + [image[16:32] for image in images], axis=0)
    others = swap(chips, "core", 1)
    scratch = [pltpu.VMEM((16, 64, 128), F32), pltpu.VMEM((2, 1792), F32), pltpu.VMEM((64, 128), F32)]
    fwd_in, fwd_mid, fwd_out, bias = kernel_call(
        forward_weight_kernel,
        "lay_out_forward_weights",
        4,
        20,
        [near(chips), near(others), tables["pick_out"]],
        [shape(1152, 768), shape(3072, 256), shape(640, 256), shape(8, 768, dtype=F32)],
        scratch,
    )
    bwd_mid, bwd_out = kernel_call(
        backward_weight_kernel,
        "lay_out_backward_weights",
        3,
        16,
        [near(chips), near(others), tables["pick_back"]],
        [shape(3072, 256), shape(288, 640)],
        scratch,
    )
    *gathered, bias, bwd_out = lax.optimization_barrier((*gathered, bias, bwd_out))
    gathered += [swap(piece, "core", 1) for piece in gathered]
    kept = [(16, 128, 128), (18, 128, 512), (2048, 640), (2048, 512), (2048, 640)]
    moved = [(128, 256), (1152, 768), (3072, 256)]
    branch, stats, lines, natural, turned, active, slope_in, slope_out = kernel_call(
        forward_kernel,
        "features_and_branch",
        27,
        26,
        [*map(near, gathered), tables["feature"], fwd_in, fwd_mid, fwd_out, bias],
        [shape(256, 128), shape(8, 256, dtype=F32), shape(256, 128)] + [shape(*dims) for dims in kept],
        [pltpu.VMEM(dims, BF) for dims in moved]
        + [pltpu.SemaphoreType.DMA((3,))]
        + [
            pltpu.VMEM((20, 128, 256), BF),
            pltpu.VMEM((4, 8, 128), F32),
            pltpu.VMEM((24, 128), F32),
            pltpu.VMEM((18, 10, 16, 128), BF),
            pltpu.VMEM((18, 6, 10, 16, 128), BF),
            pltpu.VMEM((256, 768), F32),
            pltpu.VMEM((256, 768), F32),
            pltpu.VMEM((640, 256), F32),
            pltpu.VMEM((640, 256), F32),
            pltpu.VMEM((18, 144, 128), F32),
        ],
        in_specs=[VECTOR] * 8 + [LEFT] * 3 + [VECTOR] * 2,
    )
    by_frame = lax.all_to_all(branch.reshape(16, 16, 128), ("frames", "chip", "core"), 0, 0, tiled=True)
    grads, loss = kernel_call(
        consistency_kernel,
        "data_consistency",
        2.5,
        12,
        [
            near(by_frame.reshape(256, 128)), lines, stats, mine_target, beside, other, far, others,
            tables["to_lines"], tables["to_rows"], tables["lines_again"], tables["spread"],
        ],
        [shape(512, 128), shape(8, 128, dtype=F32)],
        [pltpu.VMEM((256, 128), BF)],
    )
    by_block = lax.all_to_all(grads.reshape(16, 32, 128), ("frames", "chip", "core"), 0, 0, tiled=True)
    moved = [(288, 640), (3072, 256)]
    (parts,) = kernel_call(
        backward_kernel,
        "weight_gradients",
        27,
        30,
        [near(by_block.reshape(512, 128)), bwd_out, slope_out, active, turned, bwd_mid, slope_in, natural],
        [shape(32, 32, 128)],
        [pltpu.VMEM(dims, BF) for dims in moved]
        + [pltpu.SemaphoreType.DMA((2,))]
        + [
            pltpu.VMEM((288, 2048), BF),
            pltpu.VMEM((512, 640), F32),
            pltpu.VMEM((512, 640), F32),
            pltpu.VMEM((18, 5, 10, 16, 128), BF),
            pltpu.VMEM((8192, 128), BF),
            pltpu.VMEM((1024, 256), F32),
            pltpu.VMEM((1024, 256), F32),
            pltpu.VMEM((384, 768), F32),
            pltpu.VMEM((5, 288, 128), F32),
            pltpu.VMEM((288, 128), F32),
            pltpu.VMEM((288, 8192), BF),
            pltpu.VMEM((2048, 128), F32),
            pltpu.VMEM((16, 64, 128), F32),
            pltpu.VMEM((2, 1792), F32),
        ],
        in_specs=[VECTOR, LEFT] + [VECTOR] * 3 + [LEFT] + [VECTOR] * 2,
    )
    parts = lax.all_to_all(parts, ("frames", "half", "chip", "core"), 0, 0, tiled=True)
    shard, messages = kernel_call(
        sum_kernel,
        "sum_gradients",
        2,
        8,
        [near(parts), stats, loss],
        [shape(32, 128, dtype=F32), shape(32, 128, dtype=F32)],
        [],
    )
    shards = [shard] + [swap(shard, "frames", step) for step in (1, 2, 3)]
    messages = lax.all_to_all(messages, ("frames", "half", "chip", "core"), 0, 0, tiled=True)
    groups = (
        (conv_in, conv_mid, conv_out, conv_bias),
        (first_in, first_mid, first_out, first_bias),
        (second_in, second_mid, second_out, second_bias),
    )
    state = []
    for of_in, of_mid, of_out, of_bias in groups:
        state += [of_in[0].T, of_mid[0, 0].T, of_out[0], of_bias[0]]
    shapes = [(8, 216), (8, 1728), (2, 216), (2, 8)]
    results = kernel_call(
        update_kernel,
        "adamw",
        2,
        8,
        [*map(near, shards), near(messages), stats, *state],
        [shape(1, 1, dtype=F32)] * 3
        + [shape(*dims, dtype=F32) for dims in shapes * 3]
        + [shape(*dims, dtype=BF) for dims in shapes],
        [pltpu.VMEM((4, 32, 128), F32)] + [pltpu.VMEM(shapes[at], F32) for at in (1, 0, 2, 3)],
        out_specs=[SCALAR] * 3 + [VECTOR] * 16,
    )
    outputs = [result[0, 0] for result in results[0:3]]
    for at in range(3, 19, 4):
        of_in, of_mid, of_out, of_bias = results[at : at + 4]
        outputs += [of_in.T[None], of_mid.T[None, None], of_out[None], of_bias[None]]
    return tuple(outputs)


def specs_for(rows):
    lines = P(None, "frames", rows)
    images = P(None, "frames", rows, None, None)
    weights = [P(None, None, rows), P(None, None, None, rows), P(None, None, rows), P(None, None, rows)]
    in_specs = (images, lines, P(None, "frames"), images, *(weights * 3))
    out_specs = (P(), P(), P(), *(weights * 4))
    return in_specs, out_specs


def solution(mesh):
    frames, rows = (mesh.shape[axis] for axis in ("frames", "rows"))
    if (frames, rows) != (4, 8):
        in_specs, out_specs = specs_for("rows")
        return jax.shard_map(local, mesh=mesh, in_specs=in_specs, out_specs=out_specs, check_vma=False)
    chips = Mesh(mesh.devices.reshape(frames, 2, rows // 4, 2), ("frames", "half", "chip", "core"))
    in_specs, out_specs = specs_for(("half", "chip", "core"))
    return jax.shard_map(by_rows, mesh=chips, in_specs=in_specs, out_specs=out_specs, check_vma=False)
```

profile of v0, /device:TPU:0, one launch (start us, length us, event | category | flops | bytes accessed | tf_op | source)
XLA Modules:
  0.0 111.2 jit_solution(5268412226924626208)
XLA Ops:
  0.7 2.2 %prepare_lines.1 = (bf16[176,256]{1,0:T(8,128)(2,1)}, bf16[176,256]{1,0:T(8,128)(2,1)}, bf16[176,256]{1,0:T(8,128)(2,1)}, bf16[32,256]{1,0:T(8,128)(2,1)}) custom-call(s32[2,4]{1,0:T(2,128)} %valid.1, f32[2,4,32,128]{3,2,1,0:T(8,128)} %bitcast.91, s32[8,16]{1,0:T(8,128)} %bitcast.93, f32[2,4,32,128]{3,2,1,0:T(8,128)} %bitcast.92, ...), custom_call_target="tpu_custom_call" | custom-call | flops 2000000000 | tf_op jit(solution)/shard_map/prepare_lines/pallas_call | solution.py:1100
  2.8 4.0 %collective-permute-start.1 = (bf16[176,256]{1,0:T(8,128)(2,1)}, bf16[176,256]{1,0:T(8,128)(2,1)S(1)}, u32[]{:S(2)}, u32[]{:S(2)}) collective-permute-start(bf16[176,256]{1,0:T(8,128)(2,1)} %get-tuple-element.67), channel_id=1, source_target_pairs={{0,4},{2,6},{4,0},{6,2},{1,5},{3,7},{5,1},{7,3},{8,12},{10,14},{12... | collective-permute-start | bytes 270344 | tf_op jit(solution)/shard_map/ppermute | solution.py:1113
  6.9 1.3 %collective-permute-start.2 = (bf16[176,256]{1,0:T(8,128)(2,1)}, bf16[176,256]{1,0:T(8,128)(2,1)S(1)}, u32[]{:S(2)}, u32[]{:S(2)}) collective-permute-start(bf16[176,256]{1,0:T(8,128)(2,1)} %get-tuple-element.68), channel_id=1, source_target_pairs={{0,6},{2,4},{4,2},{6,0},{1,7},{3,5},{5,3},{7,1},{8,14},{10,12},{12... | collective-permute-start | bytes 270344 | tf_op jit(solution)/shard_map/ppermute | solution.py:1113
  8.5 0.8 slice_dynamic-update-slice_fusion.6
  9.3 5.6 %collective-permute-done.beside = bf16[176,256]{1,0:T(8,128)(2,1)S(1)} collective-permute-done((bf16[176,256]{1,0:T(8,128)(2,1)}, bf16[176,256]{1,0:T(8,128)(2,1)S(1)}, u32[]{:S(2)}, u32[]{:S(2)}) %collective-permute-start) | collective-permute-done | bytes 90144 | tf_op jit(solution)/shard_map/ppermute | solution.py:1113
  14.9 0.7 constant_dynamic-update-slice_fusion.4
  15.6 0.7 constant_dynamic-update-slice_fusion.1
  16.4 2.6 %collective-permute-start.5 = (bf16[272,256]{1,0:T(8,128)(2,1)S(1)}, bf16[272,256]{1,0:T(8,128)(2,1)S(1)}, u32[]{:S(2)}, u32[]{:S(2)}) collective-permute-start(bf16[272,256]{1,0:T(8,128)(2,1)S(1)} %get-tuple-element.72.refs_0_), channel_id=1, source_target_pairs={{0,24},{8,16},{16,8},{24,0},{1,25},{9,17},{17,9},{25,1},{2,26},{10... | collective-permute-start | bytes 417800 | tf_op jit(solution)/shard_map/ppermute | solution.py:1113
  19.9 1.0 lay_out_forward_weights.1
  21.0 0.7 lay_out_backward_weights.1
  21.7 2.0 %collective-permute-done.5.refs_3_ = bf16[272,256]{1,0:T(8,128)(2,1)S(1)} collective-permute-done((bf16[272,256]{1,0:T(8,128)(2,1)S(1)}, bf16[272,256]{1,0:T(8,128)(2,1)S(1)}, u32[]{:S(2)}, u32[]{:S(2)}) %collective-permute-start.5) | collective-permute-done | bytes 139296 | tf_op jit(solution)/shard_map/ppermute | solution.py:1113
  23.7 2.6 %collective-permute-done.4.refs_2_ = bf16[272,256]{1,0:T(8,128)(2,1)S(1)} collective-permute-done((bf16[272,256]{1,0:T(8,128)(2,1)S(1)}, bf16[272,256]{1,0:T(8,128)(2,1)S(1)}, u32[]{:S(2)}, u32[]{:S(2)}) %collective-permute-start.4) | collective-permute-done | bytes 139296 | tf_op jit(solution)/shard_map/ppermute | solution.py:1113
  28.6 19.7 %features_and_branch.1 = (bf16[256,128]{1,0:T(8,128)(2,1)S(1)}, f32[8,256]{1,0:T(8,128)S(1)}, bf16[256,128]{1,0:T(8,128)(2,1)S(1)}, bf16[16,128,128]{2,1,0:T(8,1...) custom-call(bf16[272,256]{1,0:T(8,128)(2,1)S(1)} %get-tuple-element., ...), custom_call_target="tpu_custom_call" | custom-call | flops 27000000512 | tf_op jit(solution)/shard_map/features_and_branch/pallas_call | solution.py:1100
  48.3 9.5 %all_to_all.26 = bf16[16,16,128]{2,1,0:T(8,128)(2,1)S(1)} all-to-all(bf16[16,16,128]{2,1,0:T(8,128)(2,1)S(1)} %bitcast.72), channel_id=1, replica_groups=mesh['frames'=4,'half'=2,'chip'=2,'core'=2] {'frames','chip','core'}, dimensions={0} | all-to-all | bytes 131072 | tf_op jit(solution)/shard_map/all_to_all | solution.py:1192
  57.8 0.6 data_consistency.1
  58.4 8.9 %all_to_all.27 = bf16[16,32,128]{2,1,0:T(8,128)(2,1)S(1)} all-to-all(bf16[16,32,128]{2,1,0:T(8,128)(2,1)S(1)} %bitcast.70), channel_id=1, replica_groups=mesh['frames'=4,'half'=2,'chip'=2,'core'=2] {'frames','chip','core'}, dimensions={0} | all-to-all | bytes 262144 | tf_op jit(solution)/shard_map/all_to_all | solution.py:1205
  67.4 19.1 %weight_gradients.1 = bf16[32,32,128]{2,1,0:T(8,128)(2,1)S(1)} custom-call(bf16[512,128]{1,0:T(8,128)(2,1)S(1)} %bitcast.71, bf16[288,640]{1,0:T(8,128)(2,1)S(1)} %get-tuple-element.84.bwd_out_hbm, bf16[2048,640]{1,0:T(8,128)(2,1)S(1)} %get-tuple-element.85.slope_out, bf16[2048,640]{1,0:T(8,128)(2,1)S(1)} %get-tuple-element.86.active, ...), custom_call_target="tpu_custom_call" | custom-call | flops 27000000512 | tf_op jit(solution)/shard_map/weight_gradients/pallas_call | solution.py:1100
  86.5 13.0 %all_to_all.28.parts = bf16[32,32,128]{2,1,0:T(8,128)(2,1)S(1)} all-to-all(bf16[32,32,128]{2,1,0:T(8,128)(2,1)S(1)} %weight_gradients.1), channel_id=1, replica_groups=mesh['frames'=4,'half'=2,'chip'=2,'core'=2] {'frames','half','chip','core'}, dimensions={0} | all-to-all | bytes 524288 | tf_op jit(solution)/shard_map/all_to_all | solution.py:1234
  99.6 0.8 sum_gradients.1
  100.4 2.5 %all-to-all-start.3 = ((f32[32,1,128]{2,1,0:T(1,128)}), f32[32,1,128]{2,1,0:T(1,128)S(1)}, u32[]{:S(2)}, u32[]{:S(2)}) async-start(f32[32,1,128]{2,1,0:T(1,128)} %bitcast.14), calls=%async_computation.3 | async-start | bytes 32768 | tf_op jit(solution)/shard_map/all_to_all | solution.py:1245
  102.9 2.7 %collective-permute-start.13 = (f32[32,128]{1,0:T(8,128)S(1)}, f32[32,128]{1,0:T(8,128)S(1)}, u32[]{:S(2)}, u32[]{:S(2)}) collective-permute-start(f32[32,128]{1,0:T(8,128)S(1)} %get-tuple-element.92.own), channel_id=1, source_target_pairs={{0,24},{8,16},{16,8},{24,0},{1,25},{9,17},{17,9},{25,1},{2,26},{10... | collective-permute-start | bytes 49160 | tf_op jit(solution)/shard_map/ppermute | solution.py:1113
  106.5 1.2 %collective-permute-done.13.far = f32[32,128]{1,0:T(8,128)S(1)} collective-permute-done((f32[32,128]{1,0:T(8,128)S(1)}, f32[32,128]{1,0:T(8,128)S(1)}, u32[]{:S(2)}, u32[]{:S(2)}) %collective-permute-start.13) | collective-permute-done | bytes 16416 | tf_op jit(solution)/shard_map/ppermute | solution.py:1113
  107.7 1.7 %collective-permute-done.12.mid = f32[32,128]{1,0:T(8,128)S(1)} collective-permute-done((f32[32,128]{1,0:T(8,128)S(1)}, f32[32,128]{1,0:T(8,128)S(1)}, u32[]{:S(2)}, u32[]{:S(2)}) %collective-permute-start.12) | collective-permute-done | bytes 16416 | tf_op jit(solution)/shard_map/ppermute | solution.py:1113
  110.1 0.9 adamw.1
  (65 shorter events, 5.0 us)
Async XLA Ops:
  0.7 19.3 %copy-start.15 = (bf16[64,2560]{1,0:T(8,128)(2,1)S(1)}, bf16[64,2560]{1,0:T(8,128)(2,1)}, u32[]{:S(2)}) copy-start(bf16[64,2560]{1,0:T(8,128)(2,1)} %constant.25.clone.pick_out) | copy-start | bytes 983044
  2.8 12.0 %collective-permute-start.1 = (bf16[176,256]{1,0:T(8,128)(2,1)}, bf16[176,256]{1,0:T(8,128)(2,1)S(1)}, u32[]{:S(2)}, u32[]{:S(2)}) collective-permute-start(bf16[176,256]{1,0:T(8,128)(2,1)} %get-tuple-element.67), channel_id=1, source_target_pairs={{0,4},{2,6},{4,0},{6,2},{1,5},{3,7},{5,1},{7,3},{8,12},{10,14},{12... | collective-permute-start | bytes 270344 | tf_op jit(solution)/shard_map/ppermute | solution.py:1113
  6.9 8.0 %collective-permute-start.2 = (bf16[176,256]{1,0:T(8,128)(2,1)}, bf16[176,256]{1,0:T(8,128)(2,1)S(1)}, u32[]{:S(2)}, u32[]{:S(2)}) collective-permute-start(bf16[176,256]{1,0:T(8,128)(2,1)} %get-tuple-element.68), channel_id=1, source_target_pairs={{0,6},{2,4},{4,2},{6,0},{1,7},{3,5},{5,3},{7,1},{8,14},{10,12},{12... | collective-permute-start | bytes 270344 | tf_op jit(solution)/shard_map/ppermute | solution.py:1113
  8.2 6.7 %collective-permute-start = (bf16[176,256]{1,0:T(8,128)(2,1)}, bf16[176,256]{1,0:T(8,128)(2,1)S(1)}, u32[]{:S(2)}, u32[]{:S(2)}) collective-permute-start(bf16[176,256]{1,0:T(8,128)(2,1)} %get-tuple-element.66), channel_id=1, source_target_pairs={{0,2},{2,0},{4,6},{6,4},{1,3},{3,1},{5,7},{7,5},{8,10},{10,8},{12,... | collective-permute-start | bytes 270344 | tf_op jit(solution)/shard_map/ppermute | solution.py:1113
  16.3 3.6 %collective-permute-start.6 = (bf16[320,256]{1,0:T(8,128)(2,1)S(1)}, bf16[320,256]{1,0:T(8,128)(2,1)S(1)}, u32[]{:S(2)}, u32[]{:S(2)}) collective-permute-start(bf16[320,256]{1,0:T(8,128)(2,1)S(1)} %get-tuple-element.113.own), channel_id=1, source_target_pairs={{0,1},{1,0},{2,3},{3,2},{4,5},{5,4},{6,7},{7,6},{8,9},{9,8},{10,11... | collective-permute-start | bytes 491528 | tf_op jit(solution)/shard_map/ppermute | solution.py:1113
  16.4 7.3 %collective-permute-start.5 = (bf16[272,256]{1,0:T(8,128)(2,1)S(1)}, bf16[272,256]{1,0:T(8,128)(2,1)S(1)}, u32[]{:S(2)}, u32[]{:S(2)}) collective-permute-start(bf16[272,256]{1,0:T(8,128)(2,1)S(1)} %get-tuple-element.72.refs_0_), channel_id=1, source_target_pairs={{0,24},{8,16},{16,8},{24,0},{1,25},{9,17},{17,9},{25,1},{2,26},{10... | collective-permute-start | bytes 417800 | tf_op jit(solution)/shard_map/ppermute | solution.py:1113
  19.0 7.4 %collective-permute-start.4 = (bf16[272,256]{1,0:T(8,128)(2,1)S(1)}, bf16[272,256]{1,0:T(8,128)(2,1)S(1)}, u32[]{:S(2)}, u32[]{:S(2)}) collective-permute-start(bf16[272,256]{1,0:T(8,128)(2,1)S(1)} %get-tuple-element.72.refs_0_), channel_id=1, source_target_pairs={{0,16},{8,24},{16,0},{24,8},{1,17},{9,25},{17,1},{25,9},{2,18},{10... | collective-permute-start | bytes 417800 | tf_op jit(solution)/shard_map/ppermute | solution.py:1113
  19.5 7.1 %collective-permute-start.3 = (bf16[272,256]{1,0:T(8,128)(2,1)S(1)}, bf16[272,256]{1,0:T(8,128)(2,1)S(1)}, u32[]{:S(2)}, u32[]{:S(2)}) collective-permute-start(bf16[272,256]{1,0:T(8,128)(2,1)S(1)} %get-tuple-element.72.refs_0_), channel_id=1, source_target_pairs={{0,8},{8,0},{16,24},{24,16},{1,9},{9,1},{17,25},{25,17},{2,10},{10... | collective-permute-start | bytes 417800 | tf_op jit(solution)/shard_map/ppermute | solution.py:1113
  26.5 1.4 %collective-permute-start.7 = (bf16[272,256]{1,0:T(8,128)(2,1)S(1)}, bf16[272,256]{1,0:T(8,128)(2,1)S(1)}, u32[]{:S(2)}, u32[]{:S(2)}) collective-permute-start(bf16[272,256]{1,0:T(8,128)(2,1)S(1)} %get-tuple-element.72.refs_0_), channel_id=1, source_target_pairs={{0,1},{1,0},{2,3},{3,2},{4,5},{5,4},{6,7},{7,6},{8,9},{9,8},{10,11... | collective-permute-start | bytes 417800 | tf_op jit(solution)/shard_map/ppermute | solution.py:1113
  26.5 1.6 %collective-permute-start.8 = (bf16[272,256]{1,0:T(8,128)(2,1)S(1)}, bf16[272,256]{1,0:T(8,128)(2,1)S(1)}, u32[]{:S(2)}, u32[]{:S(2)}) collective-permute-start(bf16[272,256]{1,0:T(8,128)(2,1)S(1)} %collective-permute-done.3.refs_1_), channel_id=1, source_target_pairs={{0,1},{1,0},{2,3},{3,2},{4,5},{5,4},{6,7},{7,6},{8,9},{9,8},{10,11... | collective-permute-start | bytes 417800 | tf_op jit(solution)/shard_map/ppermute | solution.py:1113
  27.0 1.4 %collective-permute-start.9 = (bf16[272,256]{1,0:T(8,128)(2,1)S(1)}, bf16[272,256]{1,0:T(8,128)(2,1)S(1)}, u32[]{:S(2)}, u32[]{:S(2)}) collective-permute-start(bf16[272,256]{1,0:T(8,128)(2,1)S(1)} %collective-permute-done.4.refs_2_), channel_id=1, source_target_pairs={{0,1},{1,0},{2,3},{3,2},{4,5},{5,4},{6,7},{7,6},{8,9},{9,8},{10,11... | collective-permute-start | bytes 417800 | tf_op jit(solution)/shard_map/ppermute | solution.py:1113
  27.1 1.6 %collective-permute-start.10 = (bf16[272,256]{1,0:T(8,128)(2,1)S(1)}, bf16[272,256]{1,0:T(8,128)(2,1)S(1)}, u32[]{:S(2)}, u32[]{:S(2)}) collective-permute-start(bf16[272,256]{1,0:T(8,128)(2,1)S(1)} %collective-permute-done.5.refs_3_), channel_id=1, source_target_pairs={{0,1},{1,0},{2,3},{3,2},{4,5},{5,4},{6,7},{7,6},{8,9},{9,8},{10,11... | collective-permute-start | bytes 417800 | tf_op jit(solution)/shard_map/ppermute | solution.py:1113
  28.6 29.2 %copy-start = (bf16[32,256]{1,0:T(8,128)(2,1)S(1)}, bf16[32,256]{1,0:T(8,128)(2,1)}, u32[]{:S(2)}) copy-start(bf16[32,256]{1,0:T(8,128)(2,1)} %get-tuple-element.69.mine_target) | copy-start | bytes 49156
  28.6 29.2 %copy-start.16 = (bf16[512,256]{1,0:T(8,128)(2,1)S(1)}, bf16[512,256]{1,0:T(8,128)(2,1)}, u32[]{:S(2)}) copy-start(bf16[512,256]{1,0:T(8,128)(2,1)} %constant.23.clone.spread) | copy-start | bytes 786436
  28.6 29.2 %copy-start.17 = (bf16[256,256]{1,0:T(8,128)(2,1)S(1)}, bf16[256,256]{1,0:T(8,128)(2,1)}, u32[]{:S(2)}) copy-start(bf16[256,256]{1,0:T(8,128)(2,1)} %constant.22.clone.to_rows) | copy-start | bytes 393220
  28.6 29.2 %copy-start.18 = (bf16[256,256]{1,0:T(8,128)(2,1)S(1)}, bf16[256,256]{1,0:T(8,128)(2,1)}, u32[]{:S(2)}) copy-start(bf16[256,256]{1,0:T(8,128)(2,1)} %constant.21.clone.lines_again) | copy-start | bytes 393220
  28.6 29.2 %copy-start.19 = (bf16[256,256]{1,0:T(8,128)(2,1)S(1)}, bf16[256,256]{1,0:T(8,128)(2,1)}, u32[]{:S(2)}) copy-start(bf16[256,256]{1,0:T(8,128)(2,1)} %constant.20.clone.to_lines) | copy-start | bytes 393220
  99.5 10.5 %copy-start.5 = (f32[1,216,8]{1,2,0:T(8,128)S(1)}, f32[1,216,8]{1,2,0:T(8,128)}, u32[]{:S(2)}) copy-start(f32[1,216,8]{1,2,0:T(8,128)} %param.33) | copy-start | bytes 20740
  99.5 10.5 %copy-start.6 = (f32[1,216,8]{1,2,0:T(8,128)S(1)}, f32[1,216,8]{1,2,0:T(8,128)}, u32[]{:S(2)}) copy-start(f32[1,216,8]{1,2,0:T(8,128)} %param.37) | copy-start | bytes 20740
  99.5 10.5 %copy-start.7 = (f32[1,2,216]{2,1,0:T(2,128)S(1)}, f32[1,2,216]{2,1,0:T(2,128)}, u32[]{:S(2)}) copy-start(f32[1,2,216]{2,1,0:T(2,128)} %param.31) | copy-start | bytes 5188
  100.4 9.6 %all-to-all-start.3 = ((f32[32,1,128]{2,1,0:T(1,128)}), f32[32,1,128]{2,1,0:T(1,128)S(1)}, u32[]{:S(2)}, u32[]{:S(2)}) async-start(f32[32,1,128]{2,1,0:T(1,128)} %bitcast.14), calls=%async_computation.3 | async-start | bytes 32768 | tf_op jit(solution)/shard_map/all_to_all | solution.py:1245
  102.9 4.7 %collective-permute-start.13 = (f32[32,128]{1,0:T(8,128)S(1)}, f32[32,128]{1,0:T(8,128)S(1)}, u32[]{:S(2)}, u32[]{:S(2)}) collective-permute-start(f32[32,128]{1,0:T(8,128)S(1)} %get-tuple-element.92.own), channel_id=1, source_target_pairs={{0,24},{8,16},{16,8},{24,0},{1,25},{9,17},{17,9},{25,1},{2,26},{10... | collective-permute-start | bytes 49160 | tf_op jit(solution)/shard_map/ppermute | solution.py:1113
  105.7 3.7 %collective-permute-start.12 = (f32[32,128]{1,0:T(8,128)S(1)}, f32[32,128]{1,0:T(8,128)S(1)}, u32[]{:S(2)}, u32[]{:S(2)}) collective-permute-start(f32[32,128]{1,0:T(8,128)S(1)} %get-tuple-element.92.own), channel_id=1, source_target_pairs={{0,16},{8,24},{16,0},{24,8},{1,17},{9,25},{17,1},{25,9},{2,18},{10... | collective-permute-start | bytes 49160 | tf_op jit(solution)/shard_map/ppermute | solution.py:1113
  106.2 3.7 %collective-permute-start.11 = (f32[32,128]{1,0:T(8,128)S(1)}, f32[32,128]{1,0:T(8,128)S(1)}, u32[]{:S(2)}, u32[]{:S(2)}) collective-permute-start(f32[32,128]{1,0:T(8,128)S(1)} %get-tuple-element.92.own), channel_id=1, source_target_pairs={{0,8},{8,0},{16,24},{24,16},{1,9},{9,1},{17,25},{25,17},{2,10},{10... | collective-permute-start | bytes 49160 | tf_op jit(solution)/shard_map/ppermute | solution.py:1113
  (11 other events, 107.1 us)
where the time goes:
time: 112 us; the launch traced here: 111 us
  Pallas kernels  45 us (40%)
  blocking collectives  31.4 us (28%)
  starting transfers between devices  16.3 us (15%)
  waiting for transfers between devices  15 us (13%)
  local copies, waits for them, and re-layouts  1.63 us (1%)
  between operations  1.15 us (1%)
    pallas_call x8, Pallas kernels, kernel_call(): pl.pallas_call(kernel, name=name, out_shape=results, in_specs=in_specs or...  45 us
    ppermute x14, waiting for transfers between devices, swap(): lax.ppermute(value, axis, [(i, i ^ bit) for i in range(lax.axis_size(axis...  15 us
    ppermute x14, starting transfers between devices, swap(): lax.ppermute(value, axis, [(i, i ^ bit) for i in range(lax.axis_size(axis...  13.7 us
    all_to_all x1, blocking collectives, by_rows(): lax.all_to_all(parts, ('frames', 'half', 'chip', 'core'), 0, 0, tiled=True)  13 us
    all_to_all x1, blocking collectives, by_rows(): lax.all_to_all(branch.reshape(16, 16, 128), ('frames', 'chip', 'core'), 0...  9.45 us
    all_to_all x1, blocking collectives, by_rows(): lax.all_to_all(grads.reshape(16, 32, 128), ('frames', 'chip', 'core'), 0,...  8.92 us
    all_to_all x1, starting transfers between devices, by_rows(): lax.all_to_all(messages, ('frames', 'half', 'chip', 'core'), 0, 0, tiled=...  2.54 us
  transfers between devices with their start and end apart: 15, of which 12 were waited for; matrix products, arithmetic and copies ran while one was open for 1% of the time, Pallas kernels for 2%

commit v1 on v0

--- a/solution.py
+++ b/solution.py
@@ -533,6 +533,17 @@
         to[80:144] = packed
 
 
+def merge_kernel(mine, beside, other, far, mine_target, column, chips):
+    flags = jnp.zeros((16, 256), F32)
+    for slot, source in enumerate((mine, beside, other, far)):
+        column[slot * 64 : slot * 64 + 64] = source[0:64]
+        flags = flags + source[64:80].astype(F32)
+        chips[slot * 64 : slot * 64 + 64] = source[80:144]
+        image = source[160:176] if slot else mine_target[16:32]
+        chips[256 + slot * 16 : 272 + slot * 16] = image
+    column[256:272] = flags.astype(BF)
+
+
 def unpack_weights(own, other, whole):
     f, half, chip, core = place()
     for side, source in enumerate((own, other)):
@@ -1128,7 +1139,7 @@
             valid_flags, kspace.reshape(2, 4, 32, 128), line_mask.reshape(8, 16), target.reshape(2, 4, 32, 128),
             tables["columns"], tables["permute"], conv_mid[0, 0].T, conv_in[0].T, conv_out[0], conv_bias[0],
         ],
-        [shape(176, 256), shape(176, 256), shape(176, 256), shape(32, 256)],
+        [pltpu.VMEM((176, 256), BF)] * 3 + [pltpu.VMEM((32, 256), BF)],
         [pltpu.VMEM((2, 80, 256), BF), pltpu.VMEM((2, 4, 16, 256), BF), pltpu.VMEM((16, 8, 128), F32)],
         in_specs=[SCALAR] + [VECTOR] * 9,
     )
@@ -1136,12 +1147,16 @@
     sent = ((mine, 1), (theirs, 2), (far, 3))
     beside, other, far = (swap(value, ("half", "chip"), step) for value, step in sent)
 
-    sources = (mine, beside, other, far)
-    flags = mine[64:80] + beside[64:80] + other[64:80] + far[64:80]
-    column = jnp.concatenate([source[0:64] for source in sources] + [flags], axis=0)
+    column, chips = kernel_call(
+        merge_kernel,
+        "merge_lines",
+        0.5,
+        8,
+        [mine, near(beside), near(other), near(far), mine_target],
+        [shape(272, 256), shape(320, 256)],
+        [],
+    )
     gathered = [column] + [swap(column, "frames", step) for step in (1, 2, 3)]
-    images = [mine_target, beside[144:176], other[144:176], far[144:176]]
-    chips = jnp.concatenate([source[80:144] for source in sources] + [image[16:32] for image in images], axis=0)
     others = swap(chips, "core", 1)
     scratch = [pltpu.VMEM((16, 64, 128), F32), pltpu.VMEM((2, 1792), F32), pltpu.VMEM((64, 128), F32)]
     fwd_in, fwd_mid, fwd_out, bias = kernel_call(

time: 112 us -> 109 us (0.973)
  local copies, waits for them, and re-layouts: 1.63 us -> 0.1 us
    unnamed x47 -> x38, local copies, waits for them, and re-layouts: 1.63 us -> 0.1 us
    pallas_call x8 -> x9, Pallas kernels: 45 us -> 44.4 us  [kernel_call(): pl.pallas_call(kernel, name=name, out_shape=results, in_specs=in_specs or...]
  transfers between devices with their start and end apart: 15 -> 15, of which waited for: 12 -> 13; matrix products, arithmetic and copies ran while one was open for 1% -> 0% of each run, Pallas kernels for 2% -> 2%
where the time goes in v1:
time: 109 us
  Pallas kernels  44.4 us (41%)
  blocking collectives  31.4 us (29%)
  starting transfers between devices  16.4 us (15%)
  waiting for transfers between devices  15.6 us (14%)
  between operations  1.11 us (1%)
    pallas_call x9, Pallas kernels, kernel_call(): pl.pallas_call(kernel, name=name, out_shape=results, in_specs=in_specs or...  44.4 us
    ppermute x14, waiting for transfers between devices, swap(): lax.ppermute(value, axis, [(i, i ^ bit) for i in range(lax.axis_size(axis...  15.6 us
    ppermute x14, starting transfers between devices, swap(): lax.ppermute(value, axis, [(i, i ^ bit) for i in range(lax.axis_size(axis...  13.9 us
    all_to_all x1, blocking collectives, by_rows(): lax.all_to_all(parts, ('frames', 'half', 'chip', 'core'), 0, 0, tiled=True)  13.1 us
    all_to_all x1, blocking collectives, by_rows(): lax.all_to_all(branch.reshape(16, 16, 128), ('frames', 'chip', 'core'), 0...  9.36 us
    all_to_all x1, blocking collectives, by_rows(): lax.all_to_all(grads.reshape(16, 32, 128), ('frames', 'chip', 'core'), 0,...  8.92 us
    all_to_all x1, starting transfers between devices, by_rows(): lax.all_to_all(messages, ('frames', 'half', 'chip', 'core'), 0, 0, tiled=...  2.54 us
  transfers between devices with their start and end apart: 15, of which 13 were waited for; matrix products, arithmetic and copies ran while one was open for 0% of the time, Pallas kernels for 2%

profile of v1, /device:TPU:0, one launch (start us, length us, event | category | flops | bytes accessed | tf_op | source)
XLA Modules:
  0.0 109.0 jit_solution(17186542518066762207)
XLA Ops:
  0.7 1.5 %prepare_lines.1 = (bf16[176,256]{1,0:T(8,128)(2,1)S(1)}, bf16[176,256]{1,0:T(8,128)(2,1)S(1)}, bf16[176,256]{1,0:T(8,128)(2,1)S(1)}, bf16[32,256]{1,0:T(8,128)(2,1)S(1)}) custom-call(s32[2,4]{1,0:T(2,128)} %valid.1, f32[2,4,32,128]{3,2,1,0:T(8,128)} %bitcast.91, s32[8,16]{1,0:T(8,128)} %bitcast.93, f32[2,4,32,128]{3,2,1,0:T(8,128)} %bitcast.92, ...), custom_call_target="tpu_custom_call" | custom-call | flops 2000000000 | tf_op jit(solution)/shard_map/prepare_lines/pallas_call | solution.py:1111
  2.1 4.1 %collective-permute-start.1 = (bf16[176,256]{1,0:T(8,128)(2,1)S(1)}, bf16[176,256]{1,0:T(8,128)(2,1)S(1)}, u32[]{:S(2)}, u32[]{:S(2)}) collective-permute-start(bf16[176,256]{1,0:T(8,128)(2,1)S(1)} %get-tuple-element.69), channel_id=1, source_target_pairs={{0,4},{2,6},{4,0},{6,2},{1,5},{3,7},{5,1},{7,3},{8,12},{10,14},{12... | collective-permute-start | bytes 270344 | tf_op jit(solution)/shard_map/ppermute | solution.py:1124
  6.2 1.3 %collective-permute-start.2 = (bf16[176,256]{1,0:T(8,128)(2,1)S(1)}, bf16[176,256]{1,0:T(8,128)(2,1)S(1)}, u32[]{:S(2)}, u32[]{:S(2)}) collective-permute-start(bf16[176,256]{1,0:T(8,128)(2,1)S(1)} %get-tuple-element.70), channel_id=1, source_target_pairs={{0,6},{2,4},{4,2},{6,0},{1,7},{3,5},{5,3},{7,1},{8,14},{10,12},{12... | collective-permute-start | bytes 270344 | tf_op jit(solution)/shard_map/ppermute | solution.py:1124
  7.8 5.6 %collective-permute-done.1.other = bf16[176,256]{1,0:T(8,128)(2,1)S(1)} collective-permute-done((bf16[176,256]{1,0:T(8,128)(2,1)S(1)}, bf16[176,256]{1,0:T(8,128)(2,1)S(1)}, u32[]{:S(2)}, u32[]{:S(2)}) %collective-permute-start.1) | collective-permute-done | bytes 90144 | tf_op jit(solution)/shard_map/ppermute | solution.py:1124
  13.5 0.6 collective-permute-done.beside
  14.2 2.6 %collective-permute-start.5 = (bf16[272,256]{1,0:T(8,128)(2,1)S(1)}, bf16[272,256]{1,0:T(8,128)(2,1)S(1)}, u32[]{:S(2)}, u32[]{:S(2)}) collective-permute-start(bf16[272,256]{1,0:T(8,128)(2,1)S(1)} %get-tuple-element.76.refs_0_), channel_id=1, source_target_pairs={{0,24},{8,16},{16,8},{24,0},{1,25},{9,17},{17,9},{25,1},{2,26},{10... | collective-permute-start | bytes 417800 | tf_op jit(solution)/shard_map/ppermute | solution.py:1124
  17.7 1.0 lay_out_forward_weights.1
  18.8 0.7 lay_out_backward_weights.1
  19.5 2.0 %collective-permute-done.5.refs_3_ = bf16[272,256]{1,0:T(8,128)(2,1)S(1)} collective-permute-done((bf16[272,256]{1,0:T(8,128)(2,1)S(1)}, bf16[272,256]{1,0:T(8,128)(2,1)S(1)}, u32[]{:S(2)}, u32[]{:S(2)}) %collective-permute-start.5) | collective-permute-done | bytes 139296 | tf_op jit(solution)/shard_map/ppermute | solution.py:1124
  21.5 2.6 %collective-permute-done.4.refs_2_ = bf16[272,256]{1,0:T(8,128)(2,1)S(1)} collective-permute-done((bf16[272,256]{1,0:T(8,128)(2,1)S(1)}, bf16[272,256]{1,0:T(8,128)(2,1)S(1)}, u32[]{:S(2)}, u32[]{:S(2)}) %collective-permute-start.4) | collective-permute-done | bytes 139296 | tf_op jit(solution)/shard_map/ppermute | solution.py:1124
  26.4 19.7 %features_and_branch.1 = (bf16[256,128]{1,0:T(8,128)(2,1)S(1)}, f32[8,256]{1,0:T(8,128)S(1)}, bf16[256,128]{1,0:T(8,128)(2,1)S(1)}, bf16[16,128,128]{2,1,0:T(8,1...) custom-call(bf16[272,256]{1,0:T(8,128)(2,1)S(1)} %get-tuple-element., ...), custom_call_target="tpu_custom_call" | custom-call | flops 27000000512 | tf_op jit(solution)/shard_map/features_and_branch/pallas_call | solution.py:1111
  46.2 9.4 %all_to_all.26 = bf16[16,16,128]{2,1,0:T(8,128)(2,1)S(1)} all-to-all(bf16[16,16,128]{2,1,0:T(8,128)(2,1)S(1)} %bitcast.72), channel_id=1, replica_groups=mesh['frames'=4,'half'=2,'chip'=2,'core'=2] {'frames','chip','core'}, dimensions={0} | all-to-all | bytes 131072 | tf_op jit(solution)/shard_map/all_to_all | solution.py:1207
  55.6 0.6 data_consistency.1
  56.2 8.9 %all_to_all.27 = bf16[16,32,128]{2,1,0:T(8,128)(2,1)S(1)} all-to-all(bf16[16,32,128]{2,1,0:T(8,128)(2,1)S(1)} %bitcast.70), channel_id=1, replica_groups=mesh['frames'=4,'half'=2,'chip'=2,'core'=2] {'frames','chip','core'}, dimensions={0} | all-to-all | bytes 262144 | tf_op jit(solution)/shard_map/all_to_all | solution.py:1220
  65.1 19.1 %weight_gradients.1 = bf16[32,32,128]{2,1,0:T(8,128)(2,1)S(1)} custom-call(bf16[512,128]{1,0:T(8,128)(2,1)S(1)} %bitcast.71, bf16[288,640]{1,0:T(8,128)(2,1)S(1)} %get-tuple-element.88.bwd_out_hbm, bf16[2048,640]{1,0:T(8,128)(2,1)S(1)} %get-tuple-element.89.slope_out, bf16[2048,640]{1,0:T(8,128)(2,1)S(1)} %get-tuple-element.90.active, ...), custom_call_target="tpu_custom_call" | custom-call | flops 27000000512 | tf_op jit(solution)/shard_map/weight_gradients/pallas_call | solution.py:1111
  84.2 13.1 %all_to_all.28.parts = bf16[32,32,128]{2,1,0:T(8,128)(2,1)S(1)} all-to-all(bf16[32,32,128]{2,1,0:T(8,128)(2,1)S(1)} %weight_gradients.1), channel_id=1, replica_groups=mesh['frames'=4,'half'=2,'chip'=2,'core'=2] {'frames','half','chip','core'}, dimensions={0} | all-to-all | bytes 524288 | tf_op jit(solution)/shard_map/all_to_all | solution.py:1249
  97.4 0.8 sum_gradients.1
  98.2 2.5 %all-to-all-start.3 = ((f32[32,1,128]{2,1,0:T(1,128)}), f32[32,1,128]{2,1,0:T(1,128)S(1)}, u32[]{:S(2)}, u32[]{:S(2)}) async-start(f32[32,1,128]{2,1,0:T(1,128)} %bitcast.14), calls=%async_computation.3 | async-start | bytes 32768 | tf_op jit(solution)/shard_map/all_to_all | solution.py:1260
  100.7 2.7 %collective-permute-start.13 = (f32[32,128]{1,0:T(8,128)S(1)}, f32[32,128]{1,0:T(8,128)S(1)}, u32[]{:S(2)}, u32[]{:S(2)}) collective-permute-start(f32[32,128]{1,0:T(8,128)S(1)} %get-tuple-element.96.own), channel_id=1, source_target_pairs={{0,24},{8,16},{16,8},{24,0},{1,25},{9,17},{17,9},{25,1},{2,26},{10... | collective-permute-start | bytes 49160 | tf_op jit(solution)/shard_map/ppermute | solution.py:1124
  103.5 0.6 collective-permute-start.12
  104.3 1.2 %collective-permute-done.13.far = f32[32,128]{1,0:T(8,128)S(1)} collective-permute-done((f32[32,128]{1,0:T(8,128)S(1)}, f32[32,128]{1,0:T(8,128)S(1)}, u32[]{:S(2)}, u32[]{:S(2)}) %collective-permute-start.13) | collective-permute-done | bytes 16416 | tf_op jit(solution)/shard_map/ppermute | solution.py:1124
  105.5 1.7 %collective-permute-done.12.mid = f32[32,128]{1,0:T(8,128)S(1)} collective-permute-done((f32[32,128]{1,0:T(8,128)S(1)}, f32[32,128]{1,0:T(8,128)S(1)}, u32[]{:S(2)}, u32[]{:S(2)}) %collective-permute-start.12) | collective-permute-done | bytes 16416 | tf_op jit(solution)/shard_map/ppermute | solution.py:1124
  107.2 0.6 collective-permute-done.11.near
  107.9 0.9 adamw.1
  (56 shorter events, 4.0 us)
Async XLA Ops:
  0.7 17.1 %copy-start.14 = (bf16[64,2560]{1,0:T(8,128)(2,1)S(1)}, bf16[64,2560]{1,0:T(8,128)(2,1)}, u32[]{:S(2)}) copy-start(bf16[64,2560]{1,0:T(8,128)(2,1)} %constant.25.clone.pick_out) | copy-start | bytes 983044
  2.1 11.3 %collective-permute-start.1 = (bf16[176,256]{1,0:T(8,128)(2,1)S(1)}, bf16[176,256]{1,0:T(8,128)(2,1)S(1)}, u32[]{:S(2)}, u32[]{:S(2)}) collective-permute-start(bf16[176,256]{1,0:T(8,128)(2,1)S(1)} %get-tuple-element.69), channel_id=1, source_target_pairs={{0,4},{2,6},{4,0},{6,2},{1,5},{3,7},{5,1},{7,3},{8,12},{10,14},{12... | collective-permute-start | bytes 270344 | tf_op jit(solution)/shard_map/ppermute | solution.py:1124
  6.2 7.2 %collective-permute-start.2 = (bf16[176,256]{1,0:T(8,128)(2,1)S(1)}, bf16[176,256]{1,0:T(8,128)(2,1)S(1)}, u32[]{:S(2)}, u32[]{:S(2)}) collective-permute-start(bf16[176,256]{1,0:T(8,128)(2,1)S(1)} %get-tuple-element.70), channel_id=1, source_target_pairs={{0,6},{2,4},{4,2},{6,0},{1,7},{3,5},{5,3},{7,1},{8,14},{10,12},{12... | collective-permute-start | bytes 270344 | tf_op jit(solution)/shard_map/ppermute | solution.py:1124
  7.6 6.5 %collective-permute-start = (bf16[176,256]{1,0:T(8,128)(2,1)S(1)}, bf16[176,256]{1,0:T(8,128)(2,1)S(1)}, u32[]{:S(2)}, u32[]{:S(2)}) collective-permute-start(bf16[176,256]{1,0:T(8,128)(2,1)S(1)} %get-tuple-element.68.mine), channel_id=1, source_target_pairs={{0,2},{2,0},{4,6},{6,4},{1,3},{3,1},{5,7},{7,5},{8,10},{10,8},{12,... | collective-permute-start | bytes 270344 | tf_op jit(solution)/shard_map/ppermute | solution.py:1124
  14.1 3.6 %collective-permute-start.6 = (bf16[320,256]{1,0:T(8,128)(2,1)S(1)}, bf16[320,256]{1,0:T(8,128)(2,1)S(1)}, u32[]{:S(2)}, u32[]{:S(2)}) collective-permute-start(bf16[320,256]{1,0:T(8,128)(2,1)S(1)} %get-tuple-element.73.own), channel_id=1, source_target_pairs={{0,1},{1,0},{2,3},{3,2},{4,5},{5,4},{6,7},{7,6},{8,9},{9,8},{10,11... | collective-permute-start | bytes 491528 | tf_op jit(solution)/shard_map/ppermute | solution.py:1124
  14.2 7.3 %collective-permute-start.5 = (bf16[272,256]{1,0:T(8,128)(2,1)S(1)}, bf16[272,256]{1,0:T(8,128)(2,1)S(1)}, u32[]{:S(2)}, u32[]{:S(2)}) collective-permute-start(bf16[272,256]{1,0:T(8,128)(2,1)S(1)} %get-tuple-element.76.refs_0_), channel_id=1, source_target_pairs={{0,24},{8,16},{16,8},{24,0},{1,25},{9,17},{17,9},{25,1},{2,26},{10... | collective-permute-start | bytes 417800 | tf_op jit(solution)/shard_map/ppermute | solution.py:1124
  16.8 7.3 %collective-permute-start.4 = (bf16[272,256]{1,0:T(8,128)(2,1)S(1)}, bf16[272,256]{1,0:T(8,128)(2,1)S(1)}, u32[]{:S(2)}, u32[]{:S(2)}) collective-permute-start(bf16[272,256]{1,0:T(8,128)(2,1)S(1)} %get-tuple-element.76.refs_0_), channel_id=1, source_target_pairs={{0,16},{8,24},{16,0},{24,8},{1,17},{9,25},{17,1},{25,9},{2,18},{10... | collective-permute-start | bytes 417800 | tf_op jit(solution)/shard_map/ppermute | solution.py:1124
  17.3 7.0 %collective-permute-start.3 = (bf16[272,256]{1,0:T(8,128)(2,1)S(1)}, bf16[272,256]{1,0:T(8,128)(2,1)S(1)}, u32[]{:S(2)}, u32[]{:S(2)}) collective-permute-start(bf16[272,256]{1,0:T(8,128)(2,1)S(1)} %get-tuple-element.76.refs_0_), channel_id=1, source_target_pairs={{0,8},{8,0},{16,24},{24,16},{1,9},{9,1},{17,25},{25,17},{2,10},{10... | collective-permute-start | bytes 417800 | tf_op jit(solution)/shard_map/ppermute | solution.py:1124
  24.3 1.4 %collective-permute-start.7 = (bf16[272,256]{1,0:T(8,128)(2,1)S(1)}, bf16[272,256]{1,0:T(8,128)(2,1)S(1)}, u32[]{:S(2)}, u32[]{:S(2)}) collective-permute-start(bf16[272,256]{1,0:T(8,128)(2,1)S(1)} %get-tuple-element.76.refs_0_), channel_id=1, source_target_pairs={{0,1},{1,0},{2,3},{3,2},{4,5},{5,4},{6,7},{7,6},{8,9},{9,8},{10,11... | collective-permute-start | bytes 417800 | tf_op jit(solution)/shard_map/ppermute | solution.py:1124
  24.3 1.6 %collective-permute-start.8 = (bf16[272,256]{1,0:T(8,128)(2,1)S(1)}, bf16[272,256]{1,0:T(8,128)(2,1)S(1)}, u32[]{:S(2)}, u32[]{:S(2)}) collective-permute-start(bf16[272,256]{1,0:T(8,128)(2,1)S(1)} %collective-permute-done.3.refs_1_), channel_id=1, source_target_pairs={{0,1},{1,0},{2,3},{3,2},{4,5},{5,4},{6,7},{7,6},{8,9},{9,8},{10,11... | collective-permute-start | bytes 417800 | tf_op jit(solution)/shard_map/ppermute | solution.py:1124
  24.8 1.4 %collective-permute-start.9 = (bf16[272,256]{1,0:T(8,128)(2,1)S(1)}, bf16[272,256]{1,0:T(8,128)(2,1)S(1)}, u32[]{:S(2)}, u32[]{:S(2)}) collective-permute-start(bf16[272,256]{1,0:T(8,128)(2,1)S(1)} %collective-permute-done.4.refs_2_), channel_id=1, source_target_pairs={{0,1},{1,0},{2,3},{3,2},{4,5},{5,4},{6,7},{7,6},{8,9},{9,8},{10,11... | collective-permute-start | bytes 417800 | tf_op jit(solution)/shard_map/ppermute | solution.py:1124
  24.8 1.6 %collective-permute-start.10 = (bf16[272,256]{1,0:T(8,128)(2,1)S(1)}, bf16[272,256]{1,0:T(8,128)(2,1)S(1)}, u32[]{:S(2)}, u32[]{:S(2)}) collective-permute-start(bf16[272,256]{1,0:T(8,128)(2,1)S(1)} %collective-permute-done.5.refs_3_), channel_id=1, source_target_pairs={{0,1},{1,0},{2,3},{3,2},{4,5},{5,4},{6,7},{7,6},{8,9},{9,8},{10,11... | collective-permute-start | bytes 417800 | tf_op jit(solution)/shard_map/ppermute | solution.py:1124
  26.4 29.1 %copy-start.15 = (bf16[512,256]{1,0:T(8,128)(2,1)S(1)}, bf16[512,256]{1,0:T(8,128)(2,1)}, u32[]{:S(2)}) copy-start(bf16[512,256]{1,0:T(8,128)(2,1)} %constant.23.clone.spread) | copy-start | bytes 786436
  26.4 29.1 %copy-start.16 = (bf16[256,256]{1,0:T(8,128)(2,1)S(1)}, bf16[256,256]{1,0:T(8,128)(2,1)}, u32[]{:S(2)}) copy-start(bf16[256,256]{1,0:T(8,128)(2,1)} %constant.22.clone.to_rows) | copy-start | bytes 393220
  26.4 29.1 %copy-start.17 = (bf16[256,256]{1,0:T(8,128)(2,1)S(1)}, bf16[256,256]{1,0:T(8,128)(2,1)}, u32[]{:S(2)}) copy-start(bf16[256,256]{1,0:T(8,128)(2,1)} %constant.21.clone.lines_again) | copy-start | bytes 393220
  26.4 29.1 %copy-start.18 = (bf16[256,256]{1,0:T(8,128)(2,1)S(1)}, bf16[256,256]{1,0:T(8,128)(2,1)}, u32[]{:S(2)}) copy-start(bf16[256,256]{1,0:T(8,128)(2,1)} %constant.20.clone.to_lines) | copy-start | bytes 393220
  97.3 10.5 %copy-start.3 = (f32[1,216,8]{1,2,0:T(8,128)S(1)}, f32[1,216,8]{1,2,0:T(8,128)}, u32[]{:S(2)}) copy-start(f32[1,216,8]{1,2,0:T(8,128)} %param.29) | copy-start | bytes 20740
  97.3 10.5 %copy-start.4 = (f32[1,216,8]{1,2,0:T(8,128)S(1)}, f32[1,216,8]{1,2,0:T(8,128)}, u32[]{:S(2)}) copy-start(f32[1,216,8]{1,2,0:T(8,128)} %param.33) | copy-start | bytes 20740
  97.3 10.5 %copy-start.5 = (f32[1,216,8]{1,2,0:T(8,128)S(1)}, f32[1,216,8]{1,2,0:T(8,128)}, u32[]{:S(2)}) copy-start(f32[1,216,8]{1,2,0:T(8,128)} %param.37) | copy-start | bytes 20740
  97.3 10.5 %copy-start.6 = (f32[1,2,216]{2,1,0:T(2,128)S(1)}, f32[1,2,216]{2,1,0:T(2,128)}, u32[]{:S(2)}) copy-start(f32[1,2,216]{2,1,0:T(2,128)} %param.31) | copy-start | bytes 5188
  98.2 9.6 %all-to-all-start.3 = ((f32[32,1,128]{2,1,0:T(1,128)}), f32[32,1,128]{2,1,0:T(1,128)S(1)}, u32[]{:S(2)}, u32[]{:S(2)}) async-start(f32[32,1,128]{2,1,0:T(1,128)} %bitcast.14), calls=%async_computation.3 | async-start | bytes 32768 | tf_op jit(solution)/shard_map/all_to_all | solution.py:1260
  100.7 4.7 %collective-permute-start.13 = (f32[32,128]{1,0:T(8,128)S(1)}, f32[32,128]{1,0:T(8,128)S(1)}, u32[]{:S(2)}, u32[]{:S(2)}) collective-permute-start(f32[32,128]{1,0:T(8,128)S(1)} %get-tuple-element.96.own), channel_id=1, source_target_pairs={{0,24},{8,16},{16,8},{24,0},{1,25},{9,17},{17,9},{25,1},{2,26},{10... | collective-permute-start | bytes 49160 | tf_op jit(solution)/shard_map/ppermute | solution.py:1124
  103.5 3.7 %collective-permute-start.12 = (f32[32,128]{1,0:T(8,128)S(1)}, f32[32,128]{1,0:T(8,128)S(1)}, u32[]{:S(2)}, u32[]{:S(2)}) collective-permute-start(f32[32,128]{1,0:T(8,128)S(1)} %get-tuple-element.96.own), channel_id=1, source_target_pairs={{0,16},{8,24},{16,0},{24,8},{1,17},{9,25},{17,1},{25,9},{2,18},{10... | collective-permute-start | bytes 49160 | tf_op jit(solution)/shard_map/ppermute | solution.py:1124
  104.0 3.7 %collective-permute-start.11 = (f32[32,128]{1,0:T(8,128)S(1)}, f32[32,128]{1,0:T(8,128)S(1)}, u32[]{:S(2)}, u32[]{:S(2)}) collective-permute-start(f32[32,128]{1,0:T(8,128)S(1)} %get-tuple-element.96.own), channel_id=1, source_target_pairs={{0,8},{8,0},{16,24},{24,16},{1,9},{9,1},{17,25},{25,17},{2,10},{10... | collective-permute-start | bytes 49160 | tf_op jit(solution)/shard_map/ppermute | solution.py:1124
  (10 other events, 96.5 us)
